TPU v7x, 128 devices: a whole 4x4x4 slice. The times are simulated.
128 devices in a mesh: layer: 2 (over core), gy: 8 (over y_lo, z), gx: 8 (over x, y_hi).
Axes of the slice: x: 4, y: 4 (y_hi: 2, y_lo: 2; y = y_hi * 2 + y_lo), z: 4, core: 2. Of those that a mesh axis runs over, the one named last changes fastest.
Arguments:
- frames: bfloat16 [2, 32, 2048, 256], P(None, 'gy', 'gx'), may hold values from -6 to 6
- hidden_init: bfloat16 [2, 32, 2048, 256], P('layer', 'gy', 'gx'), may hold values from -1 to 1
- cell_init: float32 [2, 32, 2048, 256], P('layer', 'gy', 'gx'), may hold values from -5 to 5
- conv_weight: bfloat16 [2, 4608, 1024], P('layer'), may hold values from -0.09375 to 0.09375
- conv_bias: float32 [2, 1024], replicated, may hold values from -4 to 4
Outputs:
- hidden_out: bfloat16 [2, 32, 2048, 256], P('layer', 'gy', 'gx')
- cell_out: float32 [2, 32, 2048, 256], P('layer', 'gy', 'gx')
All inputs are finite; a program needn't handle non-finite values.
Results may differ from a plain program's by a relative error of at most 0.0021.
Values may be sent and summed in bfloat16 or wider, within the bound.
No kernel may reach another device: no remote copies, remote signals or barrier semaphores. Data moves between devices by JAX's collectives and lax.ppermute only.
A program may use at most 128 MiB of HBM per device.

v0:
```python
import jax
import jax.numpy as jnp
from jax import lax
from jax.experimental import pallas as pl
from jax.experimental.pallas import tpu as pltpu
from jax.sharding import PartitionSpec as P

f32 = jnp.float32
bf16 = jnp.bfloat16
ROWS, COLS, CH, GATES = 4, 256, 256, 1024
PAD = 8
EXT = COLS + 2 * PAD
LO, HI = 16, EXT - 16
NB = 512
UNIT = 2 * ROWS * COLS * 4608 * 1024
ACC = (ROWS, EXT, GATES)
TILE = (ROWS, EXT, CH)
STACK = (3, ROWS, EXT, CH)
PAIR = (3, 2, EXT, CH)
EDGE = (20, PAD, CH)

CENTER = (3, ROWS, COLS, CH)
GROUP = CH // 2

ANYV = pl.BlockSpec(memory_space=pltpu.VMEM)
HBM = pl.BlockSpec(memory_space=pltpu.HBM)


def vm(shape, dtype):
    return pltpu.VMEM(shape, dtype)


class Chain:
    def __init__(self):
        self.mark = ()

    def __call__(self, body, outs, args, aliases=None, scratch=(), part=0.0, limit=8, far=(), far_out=()):
        flat, tree = jax.tree.flatten(list(args))
        places = jax.tree.unflatten(tree, range(len(flat)))
        aliases = {places[i]: o for i, o in (aliases or {}).items()}
        given, marks, made = len(flat), len(self.mark), len(outs)

        def kernel(*refs):
            first = given + marks
            inputs = jax.tree.unflatten(tree, refs[:given])
            return body(*inputs, *refs[first : first + made], *refs[first + made + 1 :])

        *results, mark = pl.pallas_call(
            kernel,
            in_specs=[HBM if i in far else ANYV for i in range(given)] + [ANYV] * marks,
            out_specs=[HBM if i in far_out else ANYV for i in range(made)] + [ANYV],
            out_shape=list(outs) + [vm((8, 128), f32)],
            scratch_shapes=list(scratch),
            input_output_aliases=aliases,
            compiler_params=pltpu.CompilerParams(vmem_limit_bytes=limit << 20),
            cost_estimate=pl.CostEstimate(flops=int(UNIT * part), bytes_accessed=1 << 20, transcendentals=0),
        )(*flat, *self.mark)
        self.mark = (mark,)
        return results


def far(x):
    return pltpu.with_memory_space_constraint(x, pltpu.HBM)


def core_is(k):
    return pl.when(lax.axis_index("layer") == k)


def inside(axis, step):
    at = lax.axis_index(axis) + step
    return jnp.logical_and(at >= 0, at < lax.axis_size(axis)).astype(f32)


def build(stack, r, x):
    x = x.astype(f32)
    stack[0, r] = pltpu.roll(x, 1, 0).astype(bf16)
    stack[1, r] = x.astype(bf16)
    stack[2, r] = pltpu.roll(x, EXT - 1, 0).astype(bf16)


def widen(row, left, right):
    a = left.astype(f32) * inside("gx", -1)
    b = right.astype(f32) * inside("gx", 1)
    return jnp.concatenate([a, row.astype(f32), b], axis=0)


def bare(row):
    zero = jnp.zeros((PAD, CH), f32)
    return jnp.concatenate([zero, row.astype(f32), zero], axis=0)


def build_center(stack, r, x):
    x = x.astype(f32)
    for dx, y in ((0, pltpu.roll(x, 1, 0)), (1, x), (2, pltpu.roll(x, EXT - 1, 0))):
        stack[dx, r] = y[PAD : PAD + COLS].astype(bf16)


BLOCKS = range(GATES // NB)


def block(n):
    return slice(n * NB, (n + 1) * NB) if isinstance(n, int) else pl.ds(pl.multiple_of(n * NB, NB), NB)


def each_block(body):
    def step(n, carry):
        body(n)
        return carry

    lax.fori_loop(0, GATES // NB, step, 0)


def taps(w, n, lhs, off, tap, total):
    d = jnp.dot(lhs, w[tap, off : off + 256, block(n)], preferred_element_type=f32)
    return d if total is None else total + d


def inner(acc, w, stack, off, n, r, lo, hi, add):
    c = block(n)
    total = acc[r, lo:hi, c] if add else None
    for dy in range(3):
        q = r + dy - 1
        if 0 <= q < ROWS:
            for dx in range(3):
                total = taps(w, n, stack[dx, q, lo:hi, :], off, 3 * dy + dx, total)
    acc[r, lo:hi, c] = total


ENDS = ((0, 0, 0), (ROWS - 1, 1, 2))


def outer(acc, w, parts, n, end, m=EXT):
    r, q, dy = ENDS[end]
    c = slice(n * NB, (n + 1) * NB)
    total = acc[r, 0:m, c]
    for dx in range(3):
        for stack, off in parts:
            total = taps(w, n, stack[dx, q], off, 3 * dy + dx, total)
    acc[r, 0:m, c] = total


def sigmoid(x):
    return 0.5 * jnp.tanh(0.5 * x) + 0.5


def gates_at(acc, bias, layer, r, n, at, cell):
    def gate(i):
        b = bias[layer : layer + 1, i * CH + n * GROUP : i * CH + (n + 1) * GROUP]
        return acc[r, at, i * CH + n * GROUP : i * CH + (n + 1) * GROUP] + b

    cell = sigmoid(gate(1)) * cell + sigmoid(gate(0)) * jnp.tanh(gate(3))
    return cell, sigmoid(gate(2)) * jnp.tanh(cell)


def finish(acc, bias, layer, r, n, cx, h):
    ch = slice(n * GROUP, (n + 1) * GROUP)
    for k in range(EXT // 16):
        at = slice(k * 16, (k + 1) * 16)
        new, hid = gates_at(acc, bias, layer, r, n, at, cx[r, at, ch])
        cx[r, at, ch] = new
        if k in (0, EXT // 16 - 1):
            half = lax.broadcasted_iota(jnp.int32, (16, GROUP), 0) < PAD
            kept = half if k else jnp.logical_not(half)
            hid = hid * jnp.where(kept, 1.0, inside("gx", 1 if k else -1))
        h[r, at, ch] = hid.astype(bf16)


def ends(acc, w, parts, bias, layer, cx, h):
    for n in BLOCKS:
        outer(acc, w, parts, n, 0)
    for n in BLOCKS:
        outer(acc, w, parts, n, 1)
        finish(acc, bias, layer, 0, n, cx, h)
    for n in BLOCKS:
        finish(acc, bias, layer, ROWS - 1, n, cx, h)


def finish_center(acc, bias, r, n, cx, hv, cv):
    ch = slice(n * GROUP, (n + 1) * GROUP)
    for k in range(COLS // 16):
        at = slice(k * 16, (k + 1) * 16)
        src = slice(k * 16 + PAD, (k + 1) * 16 + PAD)
        new, hid = gates_at(acc, bias, 1, r, n, at, cx[r, src, ch])
        cv[r, at, ch] = new
        hv[r, at, ch] = hid.astype(bf16)


def k_edges(fr, hid, cell, to_left, to_right, fs, hs, cs, sem):
    jobs = []
    for side, a in ((0, 0), (1, COLS - 16)):
        jobs.append((fr.at[:, :, a : a + 16, :], fs.at[side]))
        jobs.append((hid.at[0, :, a : a + 16, :], hs.at[side]))
        jobs.append((cell.at[0, :, a : a + 16, :], cs.at[side]))
    copies = [pltpu.make_async_copy(src, dst, sem.at[i]) for i, (src, dst) in enumerate(jobs)]
    for c in copies:
        c.start()
    for c in copies:
        c.wait()
    for side, out, at in ((0, to_left, slice(0, PAD)), (1, to_right, slice(PAD, 16))):
        for r in range(ROWS):
            out[r] = fs[side, 0, r, at]
            out[4 + r] = fs[side, 1, r, at]
            out[8 + r] = hs[side, r, at]
            c = cs[side, r, at]
            hi = c.astype(bf16)
            out[12 + r] = hi
            out[16 + r] = (c - hi.astype(f32)).astype(bf16)


def k_hidden(hid, w, acc, s):
    for r in range(ROWS):
        build(s, r, bare(hid[0, r]))

    def body(n):
        for r in range(ROWS):
            inner(acc, w, s, 256, n, r, LO, HI, False)

    each_block(body)


def below():
    return lax.rem(lax.axis_index("layer") + lax.axis_index("gy"), 2) == 0


def my_row():
    return jnp.where(below(), ROWS - 1, 0)


def halo(s, mine, other, make=None):
    make = make or build
    mine, other = mine.astype(f32), other.astype(f32)
    make(s, 0, jnp.where(below(), other, mine) * inside("gy", -1))
    make(s, 1, jnp.where(below(), mine, other) * inside("gy", 1))


def k_lend(hid, left, right, out):
    r = ROWS - 1 - my_row()
    out[...] = widen(hid[0, r], left[8 + r], right[8 + r]).astype(bf16)


def k_rows(fr, hid, left, right, lent, out, later):
    r = my_row()
    own = widen(hid[0, r], left[8 + r], right[8 + r])
    lent = lent[...].astype(f32)
    first = lax.axis_index("layer") == 0
    out[0] = widen(fr[0, r], left[r], right[r]).astype(bf16)
    out[1] = jnp.where(first, own, lent).astype(bf16)
    later[0] = widen(fr[1, r], left[4 + r], right[4 + r]).astype(bf16)
    later[1] = jnp.where(first, lent, own).astype(bf16)


def k_sides(hid, cell, w, left, right, acc_in, acc, cx, t):
    for r in range(ROWS):
        a = left[12 + r].astype(f32) + left[16 + r].astype(f32)
        b = right[12 + r].astype(f32) + right[16 + r].astype(f32)
        cx[r] = jnp.concatenate([a, cell[0, r], b], axis=0)
        x = widen(hid[0, r], left[8 + r], right[8 + r])
        for dx, y in ((0, pltpu.roll(x, 1, 0)), (1, x), (2, pltpu.roll(x, EXT - 1, 0))):
            t[dx, r, 0:16] = y[0:16].astype(bf16)
            t[dx, r, 16:32] = y[HI:EXT].astype(bf16)
    for n in BLOCKS:
        c = slice(n * NB, (n + 1) * NB)
        total = None
        for dy in range(3):
            m = ROWS if dy == 1 else ROWS - 1
            first = max(dy - 1, 0)
            for dx in range(3):
                lhs = t[dx, first : first + m].reshape(m * 32, CH)
                d = taps(w, n, lhs, 256, 3 * dy + dx, None)
                zero = jnp.zeros((32, NB), f32)
                if dy == 0:
                    d = jnp.concatenate([zero, d], axis=0)
                if dy == 2:
                    d = jnp.concatenate([d, zero], axis=0)
                total = d if total is None else total + d
        for r in range(ROWS):
            acc[r, 0:LO, c] = total[r * 32 : r * 32 + 16]
            acc[r, HI:EXT, c] = total[r * 32 + 16 : r * 32 + 32]


def k_frame(fr, w, left, right, acc_in, acc, s1, s):
    @core_is(0)
    def _():
        def frame(dst, i, r):
            build(dst, r, widen(fr[i, r], left[4 * i + r], right[4 * i + r]))

        for r in range(ROWS):
            frame(s, 0, r)

        def body(n):
            for r in range(ROWS):
                inner(acc, w, s, 0, n, r, 0, EXT, True)

        each_block(body)
        for r in range(ROWS):
            frame(s1, 1, r)


def k_next(s1, w, bias, acc_in, cx_in, acc_b, cx, h):
    @core_is(0)
    def _():
        for r in range(ROWS):
            inner(acc_b, w, s1, 0, 0, r, 0, EXT, False)
            finish(acc_in, bias, 0, 1 + r // 2, r % 2, cx, h)


def k_rest(s1, w, b_in, acc_b):
    @core_is(0)
    def _():
        for r in range(ROWS):
            inner(acc_b, w, s1, 0, 1, r, 0, EXT, False)


def k_first(mine, other, w, bias, cx_in, h_in, acc_in, acc, h, cx, s):
    @core_is(0)
    def _():
        halo(s.at[0], mine[0], other[0])
        halo(s.at[1], mine[1], other[1])
        ends(acc, w, ((s.at[0], 0), (s.at[1], 256)), bias, 0, cx, h)


def k_second(mine, other, w, a_in, b_in, acc_a, acc_b, s):
    def work(i, acc, off):
        halo(s, mine[i], other[i])
        for end in (0, 1):
            for n in BLOCKS:
                outer(acc, w, ((s, off),), n, end)

    @core_is(0)
    def _():
        work(0, acc_b, 0)

    @core_is(1)
    def _():
        work(1, acc_a, 256)


def k_pick(h, recv, out):
    r = my_row()

    @core_is(0)
    def _():
        out[...] = h[r]

    @core_is(1)
    def _():
        out[...] = recv[r]


def k_third(h_in, recv, w, bias, cx_in, a_in, b_in, acc_a, acc_b, cx, h, s):
    def work(src, acc, off, layer):
        build(s, 0, src[0])
        build(s, 1, src[1])
        for r in (1, 2):
            build(s, r + 1, src[r + 1])
            for n in BLOCKS:
                inner(acc, w, s, off, n, r, 0, EXT, True)
                if r == 2:
                    finish(acc, bias, layer, 1, n, cx, h)
        for n in BLOCKS:
            finish(acc, bias, layer, 2, n, cx, h)

    @core_is(0)
    def _():
        work(h_in, acc_b, 256, 0)

    @core_is(1)
    def _():
        work(recv, acc_a, 0, 1)


def k_ends(w, s, a_in, b_in, acc_a, acc_b):
    def work(acc, off):
        for n in BLOCKS:
            for r in (0, ROWS - 1):
                inner(acc, w, s, off, n, r, 0, EXT, True)

    @core_is(0)
    def _():
        work(acc_b, 256)

    @core_is(1)
    def _():
        work(acc_a, 0)


def k_nothing(x_in, x):
    pass


def k_fourth(mine, other, w, bias, cx_in, h_in, a_in, b_in, acc_a, acc_b, cx, h, out, s):
    halo(s, mine[...], other[...])

    def work(acc, off, layer):
        ends(acc, w, ((s, off),), bias, layer, cx, h)

    @core_is(0)
    def _():
        work(acc_b, 256, 0)

    @core_is(1)
    def _():
        work(acc_a, 0, 1)

    out[...] = h[my_row()]


def k_fifth(h, w, acc_in, acc, s):
    @core_is(1)
    def _():
        build_center(s, 0, h[0])
        build_center(s, 1, h[1])
        for r in range(ROWS):
            if r + 2 < ROWS:
                build_center(s, r + 2, h[r + 2])
            inner(acc, w, s, 256, 0, r, 0, COLS, False)


def k_lent(recv, out):
    out[...] = recv[my_row()]


def k_join(own, lent, out):
    core = lax.axis_index("layer")
    out[core] = own[...]
    out[1 - core] = lent[...]


def k_sixth(recv, w, s1, acc_in, acc, s):
    @core_is(1)
    def _():
        for r in range(ROWS):
            inner(acc, w, s1, 256, 1, r, 0, COLS, False)
            build_center(s, r, recv[r])
        for r in range(ROWS):
            inner(acc, w, s, 0, 0, r, 0, COLS, True)


def k_seventh(h, cx, w, bias, s, acc_in, acc, hv, cv):
    @core_is(0)
    def _():
        for r in range(ROWS):
            hv[r] = h[r].astype(f32)[PAD : PAD + COLS].astype(bf16)
            cv[r] = cx[r, PAD : PAD + COLS]

    @core_is(1)
    def _():
        for r, done in ((1, None), (2, 1), (0, 2), (3, None)):
            inner(acc, w, s, 0, 1, r, 0, COLS, True)
            if done:
                for n in BLOCKS:
                    finish_center(acc, bias, done, n, cx, hv, cv)


def k_last(mine, other, cx, w, bias, hv_in, cv_in, acc_in, acc, hv, cv, ho, co, s, sem):
    def out(r):
        return (
            pltpu.make_async_copy(hv.at[r], ho.at[0, r], sem.at[0, r]),
            pltpu.make_async_copy(cv.at[r], co.at[0, r], sem.at[1, r]),
        )

    def send(r):
        for c in out(r):
            c.start()

    for r in (1, 2):
        send(r)

    @core_is(1)
    def _():
        halo(s.at[0], mine[0], other[0], build_center)
        halo(s.at[1], mine[1], other[1], build_center)
        for end in (0, 1):
            for n in BLOCKS:
                outer(acc, w, ((s.at[0], 0), (s.at[1], 256)), n, end, COLS)
                if end:
                    finish_center(acc, bias, 0, n, cx, hv, cv)
        send(0)
        for n in BLOCKS:
            finish_center(acc, bias, ROWS - 1, n, cx, hv, cv)
        send(ROWS - 1)

    @core_is(0)
    def _():
        for r in (0, 3):
            send(r)

    for r in range(ROWS):
        for c in out(r):
            c.wait()


def swap_rows(x):
    ny, nx = lax.axis_size("gy"), lax.axis_size("gx")
    pairs = []
    for core in range(2):
        for y in range(ny):
            to = (y + 1 if (core + y) % 2 == 0 else y - 1) % ny
            pairs += [((core * ny + y) * nx + x, (core * ny + to) * nx + x) for x in range(nx)]
    return lax.ppermute(x, ("layer", "gy", "gx"), pairs)


def both_ways(axis, to_low, to_high):
    n = lax.axis_size(axis)
    from_low = lax.ppermute(to_high, axis, [(i, (i + 1) % n) for i in range(n)])
    from_high = lax.ppermute(to_low, axis, [(i, (i - 1) % n) for i in range(n)])
    return from_low, from_high


def per_device(frames, hidden_init, cell_init, conv_weight, conv_bias):
    call = Chain()
    bias = conv_bias
    frames_far, hidden_far, cell_far = far(frames), far(hidden_init), far(cell_init)
    swap = [(0, 1), (1, 0)]
    sums, tile, tile32, row = vm(ACC, f32), vm(TILE, bf16), vm(TILE, f32), vm((EXT, CH), bf16)

    edge = vm(EDGE, bf16)
    to_left, to_right = call(
        k_edges,
        [edge, edge],
        [frames_far, hidden_far, cell_far],
        far=(0, 1, 2),
        scratch=[
            pltpu.VMEM((2, 2, ROWS, 16, CH), bf16),
            pltpu.VMEM((2, ROWS, 16, CH), bf16),
            pltpu.VMEM((2, ROWS, 16, CH), f32),
            pltpu.SemaphoreType.DMA((6,)),
        ],
        part=2.0,
    )
    left, right = both_ways("gx", to_left, to_right)
    w = pltpu.with_memory_space_constraint(conv_weight[0].reshape(9, 512, GATES), pltpu.VMEM)
    (acc_a,) = call(k_hidden, [sums], [hidden_init, w], scratch=[pltpu.VMEM(STACK, bf16)], part=0.4)

    def swap_cores(x):
        return lax.ppermute(x, "layer", swap)

    def hold(x):
        return call(k_nothing, [vm(x.shape, x.dtype)], [x], aliases={0: 0})[0]

    lent = swap_cores(call(k_lend, [row], [hidden_init, left, right])[0])
    acc_a, cx = call(
        k_sides,
        [sums, tile32],
        [hidden_init, cell_init, w, left, right, acc_a],
        aliases={5: 0},
        scratch=[pltpu.VMEM((3, ROWS, 32, CH), bf16)],
        part=0.1,
    )
    two_rows = vm((2, EXT, CH), bf16)
    rows, later = call(k_rows, [two_rows, two_rows], [frames, hidden_init, left, right, lent])
    mine, mine_later = swap_rows(rows), swap_rows(later)
    stack = vm(STACK, bf16)
    acc_a, next_stack = call(
        k_frame,
        [sums, stack],
        [frames, w, left, right, acc_a],
        aliases={4: 0},
        scratch=[pltpu.VMEM(STACK, bf16)],
        part=0.45,
    )
    acc_b, cx, h = call(k_next, [sums, tile32, tile], [next_stack, w, bias, acc_a, cx], aliases={4: 1}, part=0.22)
    mine = hold(mine)
    other = swap_cores(mine)
    (acc_b,) = call(k_rest, [sums], [next_stack, w, acc_b], aliases={2: 0}, part=0.22)
    mine_later = hold(mine_later)
    other_later = swap_cores(mine_later)
    acc_a, h, cx = call(
        k_first,
        [sums, tile, tile32],
        [mine, other, w, bias, cx, h, acc_a],
        aliases={4: 2, 5: 1, 6: 0},
        scratch=[pltpu.VMEM((2,) + PAIR, bf16)],
        part=0.3,
    )

    recv = swap_cores(h)
    acc_a, acc_b = call(
        k_second,
        [sums, sums],
        [mine_later, other_later, w, acc_a, acc_b],
        aliases={3: 0, 4: 1},
        scratch=[pltpu.VMEM(PAIR, bf16)],
        part=0.5,
    )
    mine = swap_rows(call(k_pick, [row], [h, recv])[0])
    acc_a, acc_b, cx, h2, s = call(
        k_third,
        [sums, sums, tile32, tile, stack],
        [h, recv, w, bias, cx, acc_a, acc_b],
        aliases={4: 2, 5: 0, 6: 1},
        part=0.25,
    )
    mine = hold(mine)
    other = swap_cores(mine)
    acc_a, acc_b = call(k_ends, [sums, sums], [w, s, acc_a, acc_b], aliases={2: 0, 3: 1}, part=0.2)
    acc_a, acc_b, cx, h, out = call(
        k_fourth,
        [sums, sums, tile32, tile, row],
        [mine, other, w, bias, cx, h2, acc_a, acc_b],
        aliases={4: 2, 5: 3, 6: 0, 7: 1},
        scratch=[pltpu.VMEM(PAIR, bf16)],
        part=0.2,
    )

    recv = swap_cores(h)
    mine = swap_rows(out)
    acc_b, s = call(k_fifth, [sums, vm(CENTER, bf16)], [h, w, acc_b], aliases={2: 0}, part=0.22)
    mine_lent = swap_rows(call(k_lent, [row], [recv])[0])
    hv, cv = vm((ROWS, COLS, CH), bf16), vm((ROWS, COLS, CH), f32)
    acc_b, s = call(k_sixth, [sums, vm(CENTER, bf16)], [recv, w, s, acc_b], aliases={3: 0}, part=0.45)
    (mine,) = call(k_join, [two_rows], [mine, mine_lent])
    other = swap_cores(mine)
    acc_b, hid, cell = call(k_seventh, [sums, hv, cv], [h, cx, w, bias, s, acc_b], aliases={5: 0}, part=0.25)
    _, _, _, ho, co = call(
        k_last,
        [
            sums,
            hv,
            cv,
            jax.ShapeDtypeStruct((1, ROWS, COLS, CH), bf16),
            jax.ShapeDtypeStruct((1, ROWS, COLS, CH), f32),
        ],
        [mine, other, cx, w, bias, hid, cell, acc_b],
        aliases={5: 1, 6: 2, 7: 0},
        far_out=(3, 4),
        scratch=[pltpu.VMEM((2, 3, 2, COLS, CH), bf16), pltpu.SemaphoreType.DMA((2, ROWS))],
        part=0.3,
    )
    return ho, co


def solution(mesh):
    placed = (
        P(None, "gy", "gx", None),
        P("layer", "gy", "gx", None),
        P("layer", "gy", "gx", None),
        P("layer", None, None),
        P(),
    )
    return jax.shard_map(
        per_device,
        mesh=mesh,
        in_specs=placed,
        out_specs=(P("layer", "gy", "gx", None), P("layer", "gy", "gx", None)),
        check_vma=False,
    )
```

profile of v0, /device:TPU:1, one launch (start us, length us, event | category | flops | bytes accessed | tf_op | source)
XLA Modules:
  0.0 61.2 jit_solution(13629668788050946545)
XLA Ops:
  0.6 1.2 %shard_map.68 = (bf16[20,8,256]{2,1,0:T(8,128)(2,1)S(1)}, bf16[20,8,256]{2,1,0:T(8,128)(2,1)S(1)}, f32[8,128]{1,0:T(8,128)S(1)}) custom-call(bf16[2,4,256,256]{3,2,1,0:T(8,128)(2,1)} %refs_0_.11, bf16[1,4,256,256]{3,2,1,0:T(8,128)(2,1)} %refs_1_.5, f32[1,4,256,256]{3,2,1,0:T(8,128)} %refs_1_.4), custom_call_target="tpu_custom_call" | custom-call | flops 19327352832 | bytes 1048576 | tf_op jit(solution)/shard_map/pallas_call | solution.py:48
  1.8 3.8 %collective-permute-start = (bf16[20,8,256]{2,1,0:T(8,128)(2,1)S(1)}, bf16[20,8,256]{2,1,0:T(8,128)(2,1)S(1)}, u32[]{:S(2)}, u32[]{:S(2)}) collective-permute-start(bf16[20,8,256]{2,1,0:T(8,128)(2,1)S(1)} %get-tuple-element.69), channel_id=1, source_target_pairs={{0,1},{1,2},{2,3},{3,4},{4,5},{5,6},{6,7},{7,0},{8,9},{9,10},{10,1... | collective-permute-start | bytes 245768 | tf_op jit(solution)/shard_map/ppermute | solution.py:506
  5.7 2.3 %collective-permute-start.1 = (bf16[20,8,256]{2,1,0:T(8,128)(2,1)S(1)}, bf16[20,8,256]{2,1,0:T(8,128)(2,1)S(1)}, u32[]{:S(2)}, u32[]{:S(2)}) collective-permute-start(bf16[20,8,256]{2,1,0:T(8,128)(2,1)S(1)} %get-tuple-element.70), channel_id=1, source_target_pairs={{0,7},{1,0},{2,1},{3,2},{4,3},{5,4},{6,5},{7,6},{8,15},{9,8},{10,9... | collective-permute-start | bytes 245768 | tf_op jit(solution)/shard_map/ppermute | solution.py:507
  7.9 4.4 %shard_map.69 = (f32[4,272,1024]{2,1,0:T(8,128)S(1)}, f32[8,128]{1,0:T(8,128)S(1)}) custom-call(bf16[1,4,256,256]{3,2,1,0:T(8,128)(2,1)S(1)} %copy-done.1, bf16[9,512,1024]{2,1,0:T(8,128)(2,1)S(1)} %bitcast.1, f32[8,128]{1,0:T(8,128)S(1)} %get-tuple-element.71.refs_2_), custom_call_target="tpu_custom_call" | custom-call | flops 3865470464 | bytes 1048576 | tf_op jit(solution)/shard_map/pallas_call | solution.py:48
  12.4 1.1 %collective-permute-start.2 = (bf16[272,256]{1,0:T(8,128)(2,1)S(1)}, bf16[272,256]{1,0:T(8,128)(2,1)S(1)}, u32[]{:S(2)}, u32[]{:S(2)}) collective-permute-start(bf16[272,256]{1,0:T(8,128)(2,1)S(1)} %get-tuple-element.73), channel_id=1, source_target_pairs={{0,64},{64,0},{1,65},{65,1},{2,66},{66,2},{3,67},{67,3},{4,68},{68... | collective-permute-start | bytes 417800 | tf_op jit(solution)/shard_map/ppermute | solution.py:537
  13.6 0.9 %shard_map.71 = (f32[4,272,1024]{2,1,0:T(8,128)S(1)}, f32[4,272,256]{2,1,0:T(8,128)S(1)}, f32[8,128]{1,0:T(8,128)S(1)}) custom-call(bf16[1,4,256,256]{3,2,1,0:T(8,128)(2,1)S(1)} %copy-done.1, f32[1,4,256,256]{3,2,1,0:T(8,128)S(1)} %copy-done.2, bf16[9,512,1024]{2,1,0:T(8,128)(2,1)S(1)} %bitcast.2, ...), custom_call_target="tpu_custom_call", output_to_operand_aliasing={{0}: (5, {})} | custom-call | flops 966367616 | bytes 1048576 | tf_op jit(solution)/shard_map/pallas_call | solution.py:48
  14.6 0.2 copy-done.3
  14.8 0.1 shard_map.72
  14.9 4.9 %collective-permute-start.3 = (bf16[2,272,256]{2,1,0:T(8,128)(2,1)S(1)}, bf16[2,272,256]{2,1,0:T(8,128)(2,1)S(1)}, u32[]{:S(2)}, u32[]{:S(2)}) collective-permute-start(bf16[2,272,256]{2,1,0:T(8,128)(2,1)S(1)} %get-tuple-element.77), channel_id=1, source_target_pairs={{0,8},{1,9},{2,10},{3,11},{4,12},{5,13},{6,14},{7,15},{8,0},{9,1},... | collective-permute-start | bytes 835592 | tf_op jit(solution)/shard_map/ppermute | solution.py:501
  19.8 0.1 collective-permute-start.5
  19.9 0.7 %copy-done.4 = f32[2,1024]{1,0:T(2,128)S(1)} copy-done((f32[2,1024]{1,0:T(2,128)S(1)}, f32[2,1024]{1,0:T(2,128)}, u32[]{:S(2)}) %copy-start.4) | copy-done | bytes 8216
  20.6 3.1 %collective-permute-done.3.refs_0_ = bf16[2,272,256]{2,1,0:T(8,128)(2,1)S(1)} collective-permute-done((bf16[2,272,256]{2,1,0:T(8,128)(2,1)S(1)}, bf16[2,272,256]{2,1,0:T(8,128)(2,1)S(1)}, u32[]{:S(2)}, u32[]{:S(2)}) %collective-permute-start.3) | collective-permute-done | bytes 278560 | tf_op jit(solution)/shard_map/ppermute | solution.py:501
  23.7 1.2 %collective-permute-start.4 = (bf16[2,272,256]{2,1,0:T(8,128)(2,1)S(1)}, bf16[2,272,256]{2,1,0:T(8,128)(2,1)S(1)}, u32[]{:S(2)}, u32[]{:S(2)}) collective-permute-start(bf16[2,272,256]{2,1,0:T(8,128)(2,1)S(1)} %get-tuple-element.85.refs_0_), channel_id=1, source_target_pairs={{0,64},{64,0},{1,65},{65,1},{2,66},{66,2},{3,67},{67,3},{4,68},{68... | collective-permute-start | bytes 835592 | tf_op jit(solution)/shard_map/ppermute | solution.py:537
  24.9 2.4 %collective-permute-done.5.refs_0_ = bf16[2,272,256]{2,1,0:T(8,128)(2,1)S(1)} collective-permute-done((bf16[2,272,256]{2,1,0:T(8,128)(2,1)S(1)}, bf16[2,272,256]{2,1,0:T(8,128)(2,1)S(1)}, u32[]{:S(2)}, u32[]{:S(2)}) %collective-permute-start.5) | collective-permute-done | bytes 278560 | tf_op jit(solution)/shard_map/ppermute | solution.py:501
  27.4 0.1 shard_map.78
  27.5 2.6 %collective-permute-start.6 = (bf16[4,272,256]{2,1,0:T(8,128)(2,1)S(1)}, bf16[4,272,256]{2,1,0:T(8,128)(2,1)S(1)}, u32[]{:S(2)}, u32[]{:S(2)}) collective-permute-start(bf16[4,272,256]{2,1,0:T(8,128)(2,1)S(1)} %get-tuple-element.93.refs_0_), channel_id=1, source_target_pairs={{0,64},{64,0},{1,65},{65,1},{2,66},{66,2},{3,67},{67,3},{4,68},{68... | collective-permute-start | bytes 1671176 | tf_op jit(solution)/shard_map/ppermute | solution.py:537
  30.1 1.1 %shard_map.79 = (f32[4,272,1024]{2,1,0:T(8,128)S(1)}, f32[4,272,1024]{2,1,0:T(8,128)S(1)}, f32[8,128]{1,0:T(8,128)S(1)}) custom-call(bf16[2,272,256]{2,1,0:T(8,128)(2,1)S(1)} %get-tuple-element.94.refs_0_, bf16[2,272,256]{2,1,0:T(8,128)(2,1)S(1)} %collective-permute-done.7.refs_1_, ...), custom_call_target="tpu_custom_call", output_to_operand_aliasing={{0}: (3, {}), {1}: (4, {})} | custom-call | flops 4831838208 | bytes 1048576 | tf_op jit(solution)/shard_map/pallas_call | solution.py:48
  31.1 0.5 collective-permute-done.6.refs_1_
  31.7 4.7 %collective-permute-start.8 = (bf16[272,256]{1,0:T(8,128)(2,1)S(1)}, bf16[272,256]{1,0:T(8,128)(2,1)S(1)}, u32[]{:S(2)}, u32[]{:S(2)}) collective-permute-start(bf16[272,256]{1,0:T(8,128)(2,1)S(1)} %get-tuple-element.99), channel_id=1, source_target_pairs={{0,8},{1,9},{2,10},{3,11},{4,12},{5,13},{6,14},{7,15},{8,0},{9,1},... | collective-permute-start | bytes 417800 | tf_op jit(solution)/shard_map/ppermute | solution.py:501
  36.3 3.0 %shard_map.81 = (f32[4,272,1024]{2,1,0:T(8,128)S(1)}, f32[4,272,1024]{2,1,0:T(8,128)S(1)}, f32[4,272,256]{2,1,0:T(8,128)S(1)}, bf16[4,272,256]{2,1,0:T(8,128)(2,...) custom-call(bf16[4,272,256]{2,1,0:T(8,128)(2,1)S(1)} %get-tuple-elem, ...), custom_call_target="tpu_custom_call", output_to_operand_aliasing={{2}: (4, {}), {0}: (5, {}), {1}: (6, {})} | custom-call | flops 2415919104 | bytes 1048576 | tf_op jit(solution)/shard_map/pallas_call | solution.py:48
  39.4 0.1 collective-permute-start.9
  39.4 2.2 %shard_map.83 = (f32[4,272,1024]{2,1,0:T(8,128)S(1)}, f32[4,272,1024]{2,1,0:T(8,128)S(1)}, f32[8,128]{1,0:T(8,128)S(1)}) custom-call(bf16[9,512,1024]{2,1,0:T(8,128)(2,1)S(1)} %bitcast.9, bf16[3,4,272,256]{3,2,1,0:T(8,128)(2,1)S(1)} %get-tuple-element.108.refs_1_, ...), custom_call_target="tpu_custom_call", output_to_operand_aliasing={{0}: (2, {}), {1}: (3, {})} | custom-call | flops 1932735232 | bytes 1048576 | tf_op jit(solution)/shard_map/pallas_call | solution.py:48
  41.7 1.4 %shard_map.84 = (f32[4,272,1024]{2,1,0:T(8,128)S(1)}, f32[4,272,1024]{2,1,0:T(8,128)S(1)}, f32[4,272,256]{2,1,0:T(8,128)S(1)}, bf16[4,272,256]{2,1,0:T(8,128)(2,...) custom-call(bf16[272,256]{1,0:T(8,128)(2,1)S(1)} %get-tuple-element., ...), custom_call_target="tpu_custom_call", output_to_operand_aliasing={{2}: (4, {}), {3}: (5, {}), {0}: (6, {}), {1}: (7, {})} | custom-call | flops 1932735232 | bytes 1048576 | tf_op jit(solution)/shard_map/pallas_call | solution.py:48
  43.1 0.6 collective-permute-start.11
  43.7 2.9 %collective-permute-start.10 = (bf16[272,256]{1,0:T(8,128)(2,1)S(1)}, bf16[272,256]{1,0:T(8,128)(2,1)S(1)}, u32[]{:S(2)}, u32[]{:S(2)}) collective-permute-start(bf16[272,256]{1,0:T(8,128)(2,1)S(1)} %get-tuple-element.115), channel_id=1, source_target_pairs={{0,8},{1,9},{2,10},{3,11},{4,12},{5,13},{6,14},{7,15},{8,0},{9,1},... | collective-permute-start | bytes 417800 | tf_op jit(solution)/shard_map/ppermute | solution.py:501
  46.6 2.2 %shard_map.85 = (f32[4,272,1024]{2,1,0:T(8,128)S(1)}, bf16[3,4,256,256]{3,2,1,0:T(8,128)(2,1)S(1)}, f32[8,128]{1,0:T(8,128)S(1)}) custom-call(bf16[4,272,256]{2,1,0:T(8,128)(2,1)S(1)} %get-tuple-element.116.refs_0_, bf16[9,512,1024]{2,1,0:T(8,128)(2,1)S(1)} %bitcast.11, ...), custom_call_target="tpu_custom_call", output_to_operand_aliasing={{0}: (2, {})} | custom-call | flops 2126008832 | bytes 1048576 | tf_op jit(solution)/shard_map/pallas_call | solution.py:48
  48.9 0.7 %collective-permute-start.12 = (bf16[272,256]{1,0:T(8,128)(2,1)S(1)}, bf16[272,256]{1,0:T(8,128)(2,1)S(1)}, u32[]{:S(2)}, u32[]{:S(2)}) collective-permute-start(bf16[272,256]{1,0:T(8,128)(2,1)S(1)} %get-tuple-element.120), channel_id=1, source_target_pairs={{0,8},{1,9},{2,10},{3,11},{4,12},{5,13},{6,14},{7,15},{8,0},{9,1},... | collective-permute-start | bytes 417800 | tf_op jit(solution)/shard_map/ppermute | solution.py:501
  49.6 4.2 %shard_map.87 = (f32[4,272,1024]{2,1,0:T(8,128)S(1)}, bf16[3,4,256,256]{3,2,1,0:T(8,128)(2,1)S(1)}, f32[8,128]{1,0:T(8,128)S(1)}) custom-call(bf16[4,272,256]{2,1,0:T(8,128)(2,1)S(1)} %collective-permute-done.11.refs_0_, bf16[9,512,1024]{2,1,0:T(8,128)(2,1)S(1)} %bitcast.12, ...), custom_call_target="tpu_custom_call", output_to_operand_aliasing={{0}: (3, {})} | custom-call | flops 4348654592 | bytes 1048576 | tf_op jit(solution)/shard_map/pallas_call | solution.py:48
  53.8 1.1 %collective-permute-done.12.refs_1_ = bf16[272,256]{1,0:T(8,128)(2,1)S(1)} collective-permute-done((bf16[272,256]{1,0:T(8,128)(2,1)S(1)}, bf16[272,256]{1,0:T(8,128)(2,1)S(1)}, u32[]{:S(2)}, u32[]{:S(2)}) %collective-permute-start.12) | collective-permute-done | bytes 139296 | tf_op jit(solution)/shard_map/ppermute | solution.py:501
  55.0 0.1 collective-permute-start.13
  55.1 2.5 %shard_map.89 = (f32[4,272,1024]{2,1,0:T(8,128)S(1)}, bf16[4,256,256]{2,1,0:T(8,128)(2,1)S(1)}, f32[4,256,256]{2,1,0:T(8,128)S(1)}, f32[8,128]{1,0:T(8,128)S(1)}) custom-call(bf16[4,272,256]{2,1,0:T(8,128)(2,1)S(1)} %get-tuple-element.116.refs_0_, f32[4,272,256]{2,1,0:T(8,128)S(1)} %get-tuple-element.126.refs_1_.refs_2_, ...), custom_call_target="tpu_custom_call", output_to_operand_aliasing={{0}: (5, {})} | custom-call | flops 2415919104 | bytes 1048576 | tf_op jit(solution)/shard_map/pallas_call | solution.py:48
  57.6 3.5 %shard_map.90 = (f32[4,272,1024]{2,1,0:T(8,128)S(1)}, bf16[4,256,256]{2,1,0:T(8,128)(2,1)S(1)}, f32[4,256,256]{2,1,0:T(8,128)S(1)}, bf16[1,4,256,256]{3,2,1,0:T(...) custom-call(bf16[2,272,256]{2,1,0:T(8,128)(2,1)S(1)} %get-tuple-elem, ...), custom_call_target="tpu_custom_call", output_to_operand_aliasing={{1}: (5, {}), {2}: (6, {}), {0}: (7, {})} | custom-call | flops 2899102976 | bytes 1048576 | tf_op jit(solution)/shard_map/pallas_call | solution.py:48
  (29 shorter events, 0.3 us)
Async XLA Ops:
  0.6 7.3 %copy-start.1 = (bf16[1,4,256,256]{3,2,1,0:T(8,128)(2,1)S(1)}, bf16[1,4,256,256]{3,2,1,0:T(8,128)(2,1)}, u32[]{:S(2)}) copy-start(bf16[1,4,256,256]{3,2,1,0:T(8,128)(2,1)} %refs_1_.5) | copy-start | bytes 1572868
  0.6 7.3 %copy-start = (bf16[1,4608,1024]{2,1,0:T(8,128)(2,1)S(1)}, bf16[1,4608,1024]{2,1,0:T(8,128)(2,1)}, u32[]{:S(2)}) copy-start(bf16[1,4608,1024]{2,1,0:T(8,128)(2,1)} %param.8) | copy-start | bytes 28311556
  1.8 10.5 %collective-permute-start = (bf16[20,8,256]{2,1,0:T(8,128)(2,1)S(1)}, bf16[20,8,256]{2,1,0:T(8,128)(2,1)S(1)}, u32[]{:S(2)}, u32[]{:S(2)}) collective-permute-start(bf16[20,8,256]{2,1,0:T(8,128)(2,1)S(1)} %get-tuple-element.69), channel_id=1, source_target_pairs={{0,1},{1,2},{2,3},{3,4},{4,5},{5,6},{6,7},{7,0},{8,9},{9,10},{10,1... | collective-permute-start | bytes 245768 | tf_op jit(solution)/shard_map/ppermute | solution.py:506
  5.7 6.7 %collective-permute-start.1 = (bf16[20,8,256]{2,1,0:T(8,128)(2,1)S(1)}, bf16[20,8,256]{2,1,0:T(8,128)(2,1)S(1)}, u32[]{:S(2)}, u32[]{:S(2)}) collective-permute-start(bf16[20,8,256]{2,1,0:T(8,128)(2,1)S(1)} %get-tuple-element.70), channel_id=1, source_target_pairs={{0,7},{1,0},{2,1},{3,2},{4,3},{5,4},{6,5},{7,6},{8,15},{9,8},{10,9... | collective-permute-start | bytes 245768 | tf_op jit(solution)/shard_map/ppermute | solution.py:507
  7.9 5.6 %copy-start.2 = (f32[1,4,256,256]{3,2,1,0:T(8,128)S(1)}, f32[1,4,256,256]{3,2,1,0:T(8,128)}, u32[]{:S(2)}) copy-start(f32[1,4,256,256]{3,2,1,0:T(8,128)} %refs_1_.4) | copy-start | bytes 3145732
  12.4 2.1 %collective-permute-start.2 = (bf16[272,256]{1,0:T(8,128)(2,1)S(1)}, bf16[272,256]{1,0:T(8,128)(2,1)S(1)}, u32[]{:S(2)}, u32[]{:S(2)}) collective-permute-start(bf16[272,256]{1,0:T(8,128)(2,1)S(1)} %get-tuple-element.73), channel_id=1, source_target_pairs={{0,64},{64,0},{1,65},{65,1},{2,66},{66,2},{3,67},{67,3},{4,68},{68... | collective-permute-start | bytes 417800 | tf_op jit(solution)/shard_map/ppermute | solution.py:537
  13.6 1.2 %copy-start.3 = (bf16[2,4,256,256]{3,2,1,0:T(8,128)(2,1)S(1)}, bf16[2,4,256,256]{3,2,1,0:T(8,128)(2,1)}, u32[]{:S(2)}) copy-start(bf16[2,4,256,256]{3,2,1,0:T(8,128)(2,1)} %refs_0_.11) | copy-start | bytes 3145732
  14.9 8.9 %collective-permute-start.3 = (bf16[2,272,256]{2,1,0:T(8,128)(2,1)S(1)}, bf16[2,272,256]{2,1,0:T(8,128)(2,1)S(1)}, u32[]{:S(2)}, u32[]{:S(2)}) collective-permute-start(bf16[2,272,256]{2,1,0:T(8,128)(2,1)S(1)} %get-tuple-element.77), channel_id=1, source_target_pairs={{0,8},{1,9},{2,10},{3,11},{4,12},{5,13},{6,14},{7,15},{8,0},{9,1},... | collective-permute-start | bytes 835592 | tf_op jit(solution)/shard_map/ppermute | solution.py:501
  19.8 7.5 %collective-permute-start.5 = (bf16[2,272,256]{2,1,0:T(8,128)(2,1)S(1)}, bf16[2,272,256]{2,1,0:T(8,128)(2,1)S(1)}, u32[]{:S(2)}, u32[]{:S(2)}) collective-permute-start(bf16[2,272,256]{2,1,0:T(8,128)(2,1)S(1)} %get-tuple-element.88), channel_id=1, source_target_pairs={{0,8},{1,9},{2,10},{3,11},{4,12},{5,13},{6,14},{7,15},{8,0},{9,1},... | collective-permute-start | bytes 835592 | tf_op jit(solution)/shard_map/ppermute | solution.py:501
  19.9 0.7 %copy-start.4 = (f32[2,1024]{1,0:T(2,128)S(1)}, f32[2,1024]{1,0:T(2,128)}, u32[]{:S(2)}) copy-start(f32[2,1024]{1,0:T(2,128)} %refs_4_.1) | copy-start | bytes 24580
  23.7 3.7 %collective-permute-start.4 = (bf16[2,272,256]{2,1,0:T(8,128)(2,1)S(1)}, bf16[2,272,256]{2,1,0:T(8,128)(2,1)S(1)}, u32[]{:S(2)}, u32[]{:S(2)}) collective-permute-start(bf16[2,272,256]{2,1,0:T(8,128)(2,1)S(1)} %get-tuple-element.85.refs_0_), channel_id=1, source_target_pairs={{0,64},{64,0},{1,65},{65,1},{2,66},{66,2},{3,67},{67,3},{4,68},{68... | collective-permute-start | bytes 835592 | tf_op jit(solution)/shard_map/ppermute | solution.py:537
  27.3 2.8 %collective-permute-start.7 = (bf16[2,272,256]{2,1,0:T(8,128)(2,1)S(1)}, bf16[2,272,256]{2,1,0:T(8,128)(2,1)S(1)}, u32[]{:S(2)}, u32[]{:S(2)}) collective-permute-start(bf16[2,272,256]{2,1,0:T(8,128)(2,1)S(1)} %get-tuple-element.94.refs_0_), channel_id=1, source_target_pairs={{0,64},{64,0},{1,65},{65,1},{2,66},{66,2},{3,67},{67,3},{4,68},{68... | collective-permute-start | bytes 835592 | tf_op jit(solution)/shard_map/ppermute | solution.py:537
  27.5 4.1 %collective-permute-start.6 = (bf16[4,272,256]{2,1,0:T(8,128)(2,1)S(1)}, bf16[4,272,256]{2,1,0:T(8,128)(2,1)S(1)}, u32[]{:S(2)}, u32[]{:S(2)}) collective-permute-start(bf16[4,272,256]{2,1,0:T(8,128)(2,1)S(1)} %get-tuple-element.93.refs_0_), channel_id=1, source_target_pairs={{0,64},{64,0},{1,65},{65,1},{2,66},{66,2},{3,67},{67,3},{4,68},{68... | collective-permute-start | bytes 1671176 | tf_op jit(solution)/shard_map/ppermute | solution.py:537
  31.7 7.7 %collective-permute-start.8 = (bf16[272,256]{1,0:T(8,128)(2,1)S(1)}, bf16[272,256]{1,0:T(8,128)(2,1)S(1)}, u32[]{:S(2)}, u32[]{:S(2)}) collective-permute-start(bf16[272,256]{1,0:T(8,128)(2,1)S(1)} %get-tuple-element.99), channel_id=1, source_target_pairs={{0,8},{1,9},{2,10},{3,11},{4,12},{5,13},{6,14},{7,15},{8,0},{9,1},... | collective-permute-start | bytes 417800 | tf_op jit(solution)/shard_map/ppermute | solution.py:501
  39.4 2.3 %collective-permute-start.9 = (bf16[272,256]{1,0:T(8,128)(2,1)S(1)}, bf16[272,256]{1,0:T(8,128)(2,1)S(1)}, u32[]{:S(2)}, u32[]{:S(2)}) collective-permute-start(bf16[272,256]{1,0:T(8,128)(2,1)S(1)} %get-tuple-element.105.refs_0_), channel_id=1, source_target_pairs={{0,64},{64,0},{1,65},{65,1},{2,66},{66,2},{3,67},{67,3},{4,68},{68... | collective-permute-start | bytes 417800 | tf_op jit(solution)/shard_map/ppermute | solution.py:537
  43.1 5.7 %collective-permute-start.11 = (bf16[4,272,256]{2,1,0:T(8,128)(2,1)S(1)}, bf16[4,272,256]{2,1,0:T(8,128)(2,1)S(1)}, u32[]{:S(2)}, u32[]{:S(2)}) collective-permute-start(bf16[4,272,256]{2,1,0:T(8,128)(2,1)S(1)} %get-tuple-element.116.refs_0_), channel_id=1, source_target_pairs={{0,64},{64,0},{1,65},{65,1},{2,66},{66,2},{3,67},{67,3},{4,68},{68... | collective-permute-start | bytes 1671176 | tf_op jit(solution)/shard_map/ppermute | solution.py:537
  43.7 10.1 %collective-permute-start.10 = (bf16[272,256]{1,0:T(8,128)(2,1)S(1)}, bf16[272,256]{1,0:T(8,128)(2,1)S(1)}, u32[]{:S(2)}, u32[]{:S(2)}) collective-permute-start(bf16[272,256]{1,0:T(8,128)(2,1)S(1)} %get-tuple-element.115), channel_id=1, source_target_pairs={{0,8},{1,9},{2,10},{3,11},{4,12},{5,13},{6,14},{7,15},{8,0},{9,1},... | collective-permute-start | bytes 417800 | tf_op jit(solution)/shard_map/ppermute | solution.py:501
  48.9 6.1 %collective-permute-start.12 = (bf16[272,256]{1,0:T(8,128)(2,1)S(1)}, bf16[272,256]{1,0:T(8,128)(2,1)S(1)}, u32[]{:S(2)}, u32[]{:S(2)}) collective-permute-start(bf16[272,256]{1,0:T(8,128)(2,1)S(1)} %get-tuple-element.120), channel_id=1, source_target_pairs={{0,8},{1,9},{2,10},{3,11},{4,12},{5,13},{6,14},{7,15},{8,0},{9,1},... | collective-permute-start | bytes 417800 | tf_op jit(solution)/shard_map/ppermute | solution.py:501
  55.0 2.6 %collective-permute-start.13 = (bf16[2,272,256]{2,1,0:T(8,128)(2,1)S(1)}, bf16[2,272,256]{2,1,0:T(8,128)(2,1)S(1)}, u32[]{:S(2)}, u32[]{:S(2)}) collective-permute-start(bf16[2,272,256]{2,1,0:T(8,128)(2,1)S(1)} %get-tuple-element.125.refs_0_), channel_id=1, source_target_pairs={{0,64},{64,0},{1,65},{65,1},{2,66},{66,2},{3,67},{67,3},{4,68},{68... | collective-permute-start | bytes 835592 | tf_op jit(solution)/shard_map/ppermute | solution.py:537
where the time goes:
time: 61.4 us; the launch traced here: 61.2 us
  Pallas kernels  26.9 us (44%)
  starting transfers between devices  25.1 us (41%)
  waiting for transfers between devices  7.25 us (12%)
  between operations  1.03 us (2%)
  local copies, waits for them, and re-layouts  0.94 us (2%)
    pallas_call x23, Pallas kernels, __call__(): pl.pallas_call(kernel, in_specs=[HBM if i in far else ANYV for i in range...  26.9 us
    ppermute x5, starting transfers between devices, swap_rows(): return lax.ppermute(x, ('layer', 'gy', 'gx'), pairs)  13.3 us
    ppermute x5, waiting for transfers between devices, swap_rows(): return lax.ppermute(x, ('layer', 'gy', 'gx'), pairs)  6.64 us
    ppermute x7, starting transfers between devices, swap_cores(): return lax.ppermute(x, 'layer', swap)  5.69 us
    ppermute x1, starting transfers between devices, both_ways(): from_low = lax.ppermute(to_high, axis, [(i, (i + 1) % n) for i in range(n)])  3.81 us
    ppermute x1, starting transfers between devices, both_ways(): from_high = lax.ppermute(to_low, axis, [(i, (i - 1) % n) for i in range(n)])  2.28 us
  transfers between devices with their start and end apart: 14, of which 5 were waited for; matrix products, arithmetic and copies ran while one was open for 0% of the time, Pallas kernels for 34%

commit v1 on v0

--- a/solution.py
+++ b/solution.py
@@ -219,19 +219,19 @@
     each_block(body)
 
 
-def below():
-    return lax.rem(lax.axis_index("layer") + lax.axis_index("gy"), 2) == 0
-
-
-def my_row():
-    return jnp.where(below(), ROWS - 1, 0)
-
-
-def halo(s, mine, other, make=None):
+def below(flip=0):
+    return lax.rem(lax.axis_index("layer") + lax.axis_index("gy") + flip, 2) == 0
+
+
+def my_row(flip=0):
+    return jnp.where(below(flip), ROWS - 1, 0)
+
+
+def halo(s, mine, other, make=None, flip=0):
     make = make or build
     mine, other = mine.astype(f32), other.astype(f32)
-    make(s, 0, jnp.where(below(), other, mine) * inside("gy", -1))
-    make(s, 1, jnp.where(below(), mine, other) * inside("gy", 1))
+    make(s, 0, jnp.where(below(flip), other, mine) * inside("gy", -1))
+    make(s, 1, jnp.where(below(flip), mine, other) * inside("gy", 1))
 
 
 def k_lend(hid, left, right, out):
@@ -403,7 +403,7 @@
     def _():
         work(acc_a, 0, 1)
 
-    out[...] = h[my_row()]
+    out[...] = h[my_row(1)]
 
 
 def k_fifth(h, w, acc_in, acc, s):
@@ -418,7 +418,7 @@
 
 
 def k_lent(recv, out):
-    out[...] = recv[my_row()]
+    out[...] = recv[my_row(1)]
 
 
 def k_join(own, lent, out):
@@ -469,8 +469,8 @@
 
     @core_is(1)
     def _():
-        halo(s.at[0], mine[0], other[0], build_center)
-        halo(s.at[1], mine[1], other[1], build_center)
+        halo(s.at[0], mine[0], other[0], build_center, 1)
+        halo(s.at[1], mine[1], other[1], build_center, 1)
         for end in (0, 1):
             for n in BLOCKS:
                 outer(acc, w, ((s.at[0], 0), (s.at[1], 256)), n, end, COLS)
@@ -491,12 +491,12 @@
             c.wait()
 
 
-def swap_rows(x):
+def swap_rows(x, flip=0):
     ny, nx = lax.axis_size("gy"), lax.axis_size("gx")
     pairs = []
     for core in range(2):
         for y in range(ny):
-            to = (y + 1 if (core + y) % 2 == 0 else y - 1) % ny
+            to = (y + 1 if (core + y + flip) % 2 == 0 else y - 1) % ny
             pairs += [((core * ny + y) * nx + x, (core * ny + to) * nx + x) for x in range(nx)]
     return lax.ppermute(x, ("layer", "gy", "gx"), pairs)
 
@@ -605,9 +605,9 @@
     )
 
     recv = swap_cores(h)
-    mine = swap_rows(out)
+    mine = swap_rows(out, 1)
     acc_b, s = call(k_fifth, [sums, vm(CENTER, bf16)], [h, w, acc_b], aliases={2: 0}, part=0.22)
-    mine_lent = swap_rows(call(k_lent, [row], [recv])[0])
+    mine_lent = swap_rows(call(k_lent, [row], [recv])[0], 1)
     hv, cv = vm((ROWS, COLS, CH), bf16), vm((ROWS, COLS, CH), f32)
     acc_b, s = call(k_sixth, [sums, vm(CENTER, bf16)], [recv, w, s, acc_b], aliases={3: 0}, part=0.45)
     (mine,) = call(k_join, [two_rows], [mine, mine_lent])

time: 61.4 us -> 60.6 us (0.987)
  waiting for transfers between devices: 7.25 us -> 6.13 us
    ppermute x7, starting transfers between devices: 5.69 us -> 8.18 us  [swap_cores(): return lax.ppermute(x, 'layer', swap)]
    ppermute x5, starting transfers between devices: 13.3 us -> 11.2 us  [swap_rows(): return lax.ppermute(x, ('layer', 'gy', 'gx'), pairs)]
    ppermute x5, waiting for transfers between devices: 6.64 us -> 5.52 us  [swap_rows(): return lax.ppermute(x, ('layer', 'gy', 'gx'), pairs)]
  transfers between devices with their start and end apart: 14 -> 14, of which waited for: 5 -> 4; matrix products, arithmetic and copies ran while one was open for 0% -> 0% of each run, Pallas kernels for 34% -> 34%
where the time goes in v1:
time: 60.6 us; the launch traced here: 60.5 us
  Pallas kernels  26.9 us (44%)
  starting transfers between devices  25.5 us (42%)
  waiting for transfers between devices  6.13 us (10%)
  between operations  1.03 us (2%)
  local copies, waits for them, and re-layouts  0.94 us (2%)
    pallas_call x23, Pallas kernels, __call__(): pl.pallas_call(kernel, in_specs=[HBM if i in far else ANYV for i in range...  26.9 us
    ppermute x5, starting transfers between devices, swap_rows(): return lax.ppermute(x, ('layer', 'gy', 'gx'), pairs)  11.2 us
    ppermute x7, starting transfers between devices, swap_cores(): return lax.ppermute(x, 'layer', swap)  8.18 us
    ppermute x5, waiting for transfers between devices, swap_rows(): return lax.ppermute(x, ('layer', 'gy', 'gx'), pairs)  5.52 us
    ppermute x1, starting transfers between devices, both_ways(): from_low = lax.ppermute(to_high, axis, [(i, (i + 1) % n) for i in range(n)])  3.81 us
    ppermute x1, starting transfers between devices, both_ways(): from_high = lax.ppermute(to_low, axis, [(i, (i - 1) % n) for i in range(n)])  2.28 us
  transfers between devices with their start and end apart: 14, of which 4 were waited for; matrix products, arithmetic and copies ran while one was open for 0% of the time, Pallas kernels for 34%

profile of v1, /device:TPU:1, one launch (start us, length us, event | category | flops | bytes accessed | tf_op | source)
XLA Modules:
  0.0 60.5 jit_solution(17397722744257443792)
XLA Ops:
  0.6 1.2 %shard_map.68 = (bf16[20,8,256]{2,1,0:T(8,128)(2,1)S(1)}, bf16[20,8,256]{2,1,0:T(8,128)(2,1)S(1)}, f32[8,128]{1,0:T(8,128)S(1)}) custom-call(bf16[2,4,256,256]{3,2,1,0:T(8,128)(2,1)} %refs_0_.11, bf16[1,4,256,256]{3,2,1,0:T(8,128)(2,1)} %refs_1_.5, f32[1,4,256,256]{3,2,1,0:T(8,128)} %refs_1_.4), custom_call_target="tpu_custom_call" | custom-call | flops 19327352832 | bytes 1048576 | tf_op jit(solution)/shard_map/pallas_call | solution.py:48
  1.8 3.8 %collective-permute-start = (bf16[20,8,256]{2,1,0:T(8,128)(2,1)S(1)}, bf16[20,8,256]{2,1,0:T(8,128)(2,1)S(1)}, u32[]{:S(2)}, u32[]{:S(2)}) collective-permute-start(bf16[20,8,256]{2,1,0:T(8,128)(2,1)S(1)} %get-tuple-element.69), channel_id=1, source_target_pairs={{0,1},{1,2},{2,3},{3,4},{4,5},{5,6},{6,7},{7,0},{8,9},{9,10},{10,1... | collective-permute-start | bytes 245768 | tf_op jit(solution)/shard_map/ppermute | solution.py:506
  5.7 2.3 %collective-permute-start.1 = (bf16[20,8,256]{2,1,0:T(8,128)(2,1)S(1)}, bf16[20,8,256]{2,1,0:T(8,128)(2,1)S(1)}, u32[]{:S(2)}, u32[]{:S(2)}) collective-permute-start(bf16[20,8,256]{2,1,0:T(8,128)(2,1)S(1)} %get-tuple-element.70), channel_id=1, source_target_pairs={{0,7},{1,0},{2,1},{3,2},{4,3},{5,4},{6,5},{7,6},{8,15},{9,8},{10,9... | collective-permute-start | bytes 245768 | tf_op jit(solution)/shard_map/ppermute | solution.py:507
  7.9 4.4 %shard_map.69 = (f32[4,272,1024]{2,1,0:T(8,128)S(1)}, f32[8,128]{1,0:T(8,128)S(1)}) custom-call(bf16[1,4,256,256]{3,2,1,0:T(8,128)(2,1)S(1)} %copy-done.1, bf16[9,512,1024]{2,1,0:T(8,128)(2,1)S(1)} %bitcast.1, f32[8,128]{1,0:T(8,128)S(1)} %get-tuple-element.71.refs_2_), custom_call_target="tpu_custom_call" | custom-call | flops 3865470464 | bytes 1048576 | tf_op jit(solution)/shard_map/pallas_call | solution.py:48
  12.4 1.1 %collective-permute-start.2 = (bf16[272,256]{1,0:T(8,128)(2,1)S(1)}, bf16[272,256]{1,0:T(8,128)(2,1)S(1)}, u32[]{:S(2)}, u32[]{:S(2)}) collective-permute-start(bf16[272,256]{1,0:T(8,128)(2,1)S(1)} %get-tuple-element.73), channel_id=1, source_target_pairs={{0,64},{64,0},{1,65},{65,1},{2,66},{66,2},{3,67},{67,3},{4,68},{68... | collective-permute-start | bytes 417800 | tf_op jit(solution)/shard_map/ppermute | solution.py:537
  13.6 0.9 %shard_map.71 = (f32[4,272,1024]{2,1,0:T(8,128)S(1)}, f32[4,272,256]{2,1,0:T(8,128)S(1)}, f32[8,128]{1,0:T(8,128)S(1)}) custom-call(bf16[1,4,256,256]{3,2,1,0:T(8,128)(2,1)S(1)} %copy-done.1, f32[1,4,256,256]{3,2,1,0:T(8,128)S(1)} %copy-done.2, bf16[9,512,1024]{2,1,0:T(8,128)(2,1)S(1)} %bitcast.2, ...), custom_call_target="tpu_custom_call", output_to_operand_aliasing={{0}: (5, {})} | custom-call | flops 966367616 | bytes 1048576 | tf_op jit(solution)/shard_map/pallas_call | solution.py:48
  14.5 0.1 collective-permute-done.2.refs_4_
  14.6 0.2 copy-done.3
  14.8 0.1 shard_map.72
  14.9 4.9 %collective-permute-start.3 = (bf16[2,272,256]{2,1,0:T(8,128)(2,1)S(1)}, bf16[2,272,256]{2,1,0:T(8,128)(2,1)S(1)}, u32[]{:S(2)}, u32[]{:S(2)}) collective-permute-start(bf16[2,272,256]{2,1,0:T(8,128)(2,1)S(1)} %get-tuple-element.77), channel_id=1, source_target_pairs={{0,8},{1,9},{2,10},{3,11},{4,12},{5,13},{6,14},{7,15},{8,0},{9,1},... | collective-permute-start | bytes 835592 | tf_op jit(solution)/shard_map/ppermute | solution.py:501
  19.8 0.1 collective-permute-start.5
  19.9 0.7 %copy-done.4 = f32[2,1024]{1,0:T(2,128)S(1)} copy-done((f32[2,1024]{1,0:T(2,128)S(1)}, f32[2,1024]{1,0:T(2,128)}, u32[]{:S(2)}) %copy-start.4) | copy-done | bytes 8216
  20.6 3.1 %collective-permute-done.3.refs_0_ = bf16[2,272,256]{2,1,0:T(8,128)(2,1)S(1)} collective-permute-done((bf16[2,272,256]{2,1,0:T(8,128)(2,1)S(1)}, bf16[2,272,256]{2,1,0:T(8,128)(2,1)S(1)}, u32[]{:S(2)}, u32[]{:S(2)}) %collective-permute-start.3) | collective-permute-done | bytes 278560 | tf_op jit(solution)/shard_map/ppermute | solution.py:501
  23.7 1.2 %collective-permute-start.4 = (bf16[2,272,256]{2,1,0:T(8,128)(2,1)S(1)}, bf16[2,272,256]{2,1,0:T(8,128)(2,1)S(1)}, u32[]{:S(2)}, u32[]{:S(2)}) collective-permute-start(bf16[2,272,256]{2,1,0:T(8,128)(2,1)S(1)} %get-tuple-element.85.refs_0_), channel_id=1, source_target_pairs={{0,64},{64,0},{1,65},{65,1},{2,66},{66,2},{3,67},{67,3},{4,68},{68... | collective-permute-start | bytes 835592 | tf_op jit(solution)/shard_map/ppermute | solution.py:537
  24.9 2.4 %collective-permute-done.5.refs_0_ = bf16[2,272,256]{2,1,0:T(8,128)(2,1)S(1)} collective-permute-done((bf16[2,272,256]{2,1,0:T(8,128)(2,1)S(1)}, bf16[2,272,256]{2,1,0:T(8,128)(2,1)S(1)}, u32[]{:S(2)}, u32[]{:S(2)}) %collective-permute-start.5) | collective-permute-done | bytes 278560 | tf_op jit(solution)/shard_map/ppermute | solution.py:501
  27.3 0.1 collective-permute-start.7
  27.4 0.1 shard_map.78
  27.5 2.6 %collective-permute-start.6 = (bf16[4,272,256]{2,1,0:T(8,128)(2,1)S(1)}, bf16[4,272,256]{2,1,0:T(8,128)(2,1)S(1)}, u32[]{:S(2)}, u32[]{:S(2)}) collective-permute-start(bf16[4,272,256]{2,1,0:T(8,128)(2,1)S(1)} %get-tuple-element.93.refs_0_), channel_id=1, source_target_pairs={{0,64},{64,0},{1,65},{65,1},{2,66},{66,2},{3,67},{67,3},{4,68},{68... | collective-permute-start | bytes 1671176 | tf_op jit(solution)/shard_map/ppermute | solution.py:537
  30.1 1.1 %shard_map.79 = (f32[4,272,1024]{2,1,0:T(8,128)S(1)}, f32[4,272,1024]{2,1,0:T(8,128)S(1)}, f32[8,128]{1,0:T(8,128)S(1)}) custom-call(bf16[2,272,256]{2,1,0:T(8,128)(2,1)S(1)} %get-tuple-element.94.refs_0_, bf16[2,272,256]{2,1,0:T(8,128)(2,1)S(1)} %collective-permute-done.7.refs_1_, ...), custom_call_target="tpu_custom_call", output_to_operand_aliasing={{0}: (3, {}), {1}: (4, {})} | custom-call | flops 4831838208 | bytes 1048576 | tf_op jit(solution)/shard_map/pallas_call | solution.py:48
  31.1 0.5 collective-permute-done.6.refs_1_
  31.7 4.7 %collective-permute-start.8 = (bf16[272,256]{1,0:T(8,128)(2,1)S(1)}, bf16[272,256]{1,0:T(8,128)(2,1)S(1)}, u32[]{:S(2)}, u32[]{:S(2)}) collective-permute-start(bf16[272,256]{1,0:T(8,128)(2,1)S(1)} %get-tuple-element.99), channel_id=1, source_target_pairs={{0,8},{1,9},{2,10},{3,11},{4,12},{5,13},{6,14},{7,15},{8,0},{9,1},... | collective-permute-start | bytes 417800 | tf_op jit(solution)/shard_map/ppermute | solution.py:501
  36.3 3.0 %shard_map.81 = (f32[4,272,1024]{2,1,0:T(8,128)S(1)}, f32[4,272,1024]{2,1,0:T(8,128)S(1)}, f32[4,272,256]{2,1,0:T(8,128)S(1)}, bf16[4,272,256]{2,1,0:T(8,128)(2,...) custom-call(bf16[4,272,256]{2,1,0:T(8,128)(2,1)S(1)} %get-tuple-elem, ...), custom_call_target="tpu_custom_call", output_to_operand_aliasing={{2}: (4, {}), {0}: (5, {}), {1}: (6, {})} | custom-call | flops 2415919104 | bytes 1048576 | tf_op jit(solution)/shard_map/pallas_call | solution.py:48
  39.4 0.1 collective-permute-start.9
  39.4 2.2 %shard_map.83 = (f32[4,272,1024]{2,1,0:T(8,128)S(1)}, f32[4,272,1024]{2,1,0:T(8,128)S(1)}, f32[8,128]{1,0:T(8,128)S(1)}) custom-call(bf16[9,512,1024]{2,1,0:T(8,128)(2,1)S(1)} %bitcast.9, bf16[3,4,272,256]{3,2,1,0:T(8,128)(2,1)S(1)} %get-tuple-element.108.refs_1_, ...), custom_call_target="tpu_custom_call", output_to_operand_aliasing={{0}: (2, {}), {1}: (3, {})} | custom-call | flops 1932735232 | bytes 1048576 | tf_op jit(solution)/shard_map/pallas_call | solution.py:48
  41.7 1.4 %shard_map.84 = (f32[4,272,1024]{2,1,0:T(8,128)S(1)}, f32[4,272,1024]{2,1,0:T(8,128)S(1)}, f32[4,272,256]{2,1,0:T(8,128)S(1)}, bf16[4,272,256]{2,1,0:T(8,128)(2,...) custom-call(bf16[272,256]{1,0:T(8,128)(2,1)S(1)} %get-tuple-element., ...), custom_call_target="tpu_custom_call", output_to_operand_aliasing={{2}: (4, {}), {3}: (5, {}), {0}: (6, {}), {1}: (7, {})} | custom-call | flops 1932735232 | bytes 1048576 | tf_op jit(solution)/shard_map/pallas_call | solution.py:48
  43.1 0.6 collective-permute-start.11
  43.7 2.2 %shard_map.85 = (f32[4,272,1024]{2,1,0:T(8,128)S(1)}, bf16[3,4,256,256]{3,2,1,0:T(8,128)(2,1)S(1)}, f32[8,128]{1,0:T(8,128)S(1)}) custom-call(bf16[4,272,256]{2,1,0:T(8,128)(2,1)S(1)} %get-tuple-element.116.refs_0_, bf16[9,512,1024]{2,1,0:T(8,128)(2,1)S(1)} %bitcast.11, ...), custom_call_target="tpu_custom_call", output_to_operand_aliasing={{0}: (2, {})} | custom-call | flops 2126008832 | bytes 1048576 | tf_op jit(solution)/shard_map/pallas_call | solution.py:48
  45.9 1.5 %collective-permute-start.12 = (bf16[272,256]{1,0:T(8,128)(2,1)S(1)}, bf16[272,256]{1,0:T(8,128)(2,1)S(1)}, u32[]{:S(2)}, u32[]{:S(2)}) collective-permute-start(bf16[272,256]{1,0:T(8,128)(2,1)S(1)} %get-tuple-element.120), channel_id=1, source_target_pairs={{0,56},{1,57},{2,58},{3,59},{4,60},{5,61},{6,62},{7,63},{8,16},{9,... | collective-permute-start | bytes 417800 | tf_op jit(solution)/shard_map/ppermute | solution.py:501
  47.5 4.2 %shard_map.87 = (f32[4,272,1024]{2,1,0:T(8,128)S(1)}, bf16[3,4,256,256]{3,2,1,0:T(8,128)(2,1)S(1)}, f32[8,128]{1,0:T(8,128)S(1)}) custom-call(bf16[4,272,256]{2,1,0:T(8,128)(2,1)S(1)} %collective-permute-done.11.refs_0_, bf16[9,512,1024]{2,1,0:T(8,128)(2,1)S(1)} %bitcast.12, ...), custom_call_target="tpu_custom_call", output_to_operand_aliasing={{0}: (3, {})} | custom-call | flops 4348654592 | bytes 1048576 | tf_op jit(solution)/shard_map/pallas_call | solution.py:48
  51.8 2.6 %collective-permute-start.13 = (bf16[2,272,256]{2,1,0:T(8,128)(2,1)S(1)}, bf16[2,272,256]{2,1,0:T(8,128)(2,1)S(1)}, u32[]{:S(2)}, u32[]{:S(2)}) collective-permute-start(bf16[2,272,256]{2,1,0:T(8,128)(2,1)S(1)} %get-tuple-element.125.refs_0_), channel_id=1, source_target_pairs={{0,64},{64,0},{1,65},{65,1},{2,66},{66,2},{3,67},{67,3},{4,68},{68... | collective-permute-start | bytes 835592 | tf_op jit(solution)/shard_map/ppermute | solution.py:537
  54.4 2.4 %shard_map.89 = (f32[4,272,1024]{2,1,0:T(8,128)S(1)}, bf16[4,256,256]{2,1,0:T(8,128)(2,1)S(1)}, f32[4,256,256]{2,1,0:T(8,128)S(1)}, f32[8,128]{1,0:T(8,128)S(1)}) custom-call(bf16[4,272,256]{2,1,0:T(8,128)(2,1)S(1)} %get-tuple-element.116.refs_0_, f32[4,272,256]{2,1,0:T(8,128)S(1)} %get-tuple-element.126.refs_1_.refs_2_, ...), custom_call_target="tpu_custom_call", output_to_operand_aliasing={{0}: (5, {})} | custom-call | flops 2415919104 | bytes 1048576 | tf_op jit(solution)/shard_map/pallas_call | solution.py:48
  56.8 3.5 %shard_map.90 = (f32[4,272,1024]{2,1,0:T(8,128)S(1)}, bf16[4,256,256]{2,1,0:T(8,128)(2,1)S(1)}, f32[4,256,256]{2,1,0:T(8,128)S(1)}, bf16[1,4,256,256]{3,2,1,0:T(...) custom-call(bf16[2,272,256]{2,1,0:T(8,128)(2,1)S(1)} %get-tuple-elem, ...), custom_call_target="tpu_custom_call", output_to_operand_aliasing={{1}: (5, {}), {2}: (6, {}), {0}: (7, {})} | custom-call | flops 2899102976 | bytes 1048576 | tf_op jit(solution)/shard_map/pallas_call | solution.py:48
  (29 shorter events, 0.2 us)
Async XLA Ops:
  0.6 7.3 %copy-start.1 = (bf16[1,4,256,256]{3,2,1,0:T(8,128)(2,1)S(1)}, bf16[1,4,256,256]{3,2,1,0:T(8,128)(2,1)}, u32[]{:S(2)}) copy-start(bf16[1,4,256,256]{3,2,1,0:T(8,128)(2,1)} %refs_1_.5) | copy-start | bytes 1572868
  0.6 7.3 %copy-start = (bf16[1,4608,1024]{2,1,0:T(8,128)(2,1)S(1)}, bf16[1,4608,1024]{2,1,0:T(8,128)(2,1)}, u32[]{:S(2)}) copy-start(bf16[1,4608,1024]{2,1,0:T(8,128)(2,1)} %param.8) | copy-start | bytes 28311556
  1.8 10.5 %collective-permute-start = (bf16[20,8,256]{2,1,0:T(8,128)(2,1)S(1)}, bf16[20,8,256]{2,1,0:T(8,128)(2,1)S(1)}, u32[]{:S(2)}, u32[]{:S(2)}) collective-permute-start(bf16[20,8,256]{2,1,0:T(8,128)(2,1)S(1)} %get-tuple-element.69), channel_id=1, source_target_pairs={{0,1},{1,2},{2,3},{3,4},{4,5},{5,6},{6,7},{7,0},{8,9},{9,10},{10,1... | collective-permute-start | bytes 245768 | tf_op jit(solution)/shard_map/ppermute | solution.py:506
  5.7 6.7 %collective-permute-start.1 = (bf16[20,8,256]{2,1,0:T(8,128)(2,1)S(1)}, bf16[20,8,256]{2,1,0:T(8,128)(2,1)S(1)}, u32[]{:S(2)}, u32[]{:S(2)}) collective-permute-start(bf16[20,8,256]{2,1,0:T(8,128)(2,1)S(1)} %get-tuple-element.70), channel_id=1, source_target_pairs={{0,7},{1,0},{2,1},{3,2},{4,3},{5,4},{6,5},{7,6},{8,15},{9,8},{10,9... | collective-permute-start | bytes 245768 | tf_op jit(solution)/shard_map/ppermute | solution.py:507
  7.9 5.6 %copy-start.2 = (f32[1,4,256,256]{3,2,1,0:T(8,128)S(1)}, f32[1,4,256,256]{3,2,1,0:T(8,128)}, u32[]{:S(2)}) copy-start(f32[1,4,256,256]{3,2,1,0:T(8,128)} %refs_1_.4) | copy-start | bytes 3145732
  12.4 2.1 %collective-permute-start.2 = (bf16[272,256]{1,0:T(8,128)(2,1)S(1)}, bf16[272,256]{1,0:T(8,128)(2,1)S(1)}, u32[]{:S(2)}, u32[]{:S(2)}) collective-permute-start(bf16[272,256]{1,0:T(8,128)(2,1)S(1)} %get-tuple-element.73), channel_id=1, source_target_pairs={{0,64},{64,0},{1,65},{65,1},{2,66},{66,2},{3,67},{67,3},{4,68},{68... | collective-permute-start | bytes 417800 | tf_op jit(solution)/shard_map/ppermute | solution.py:537
  13.6 1.2 %copy-start.3 = (bf16[2,4,256,256]{3,2,1,0:T(8,128)(2,1)S(1)}, bf16[2,4,256,256]{3,2,1,0:T(8,128)(2,1)}, u32[]{:S(2)}) copy-start(bf16[2,4,256,256]{3,2,1,0:T(8,128)(2,1)} %refs_0_.11) | copy-start | bytes 3145732
  14.9 8.9 %collective-permute-start.3 = (bf16[2,272,256]{2,1,0:T(8,128)(2,1)S(1)}, bf16[2,272,256]{2,1,0:T(8,128)(2,1)S(1)}, u32[]{:S(2)}, u32[]{:S(2)}) collective-permute-start(bf16[2,272,256]{2,1,0:T(8,128)(2,1)S(1)} %get-tuple-element.77), channel_id=1, source_target_pairs={{0,8},{1,9},{2,10},{3,11},{4,12},{5,13},{6,14},{7,15},{8,0},{9,1},... | collective-permute-start | bytes 835592 | tf_op jit(solution)/shard_map/ppermute | solution.py:501
  19.8 7.5 %collective-permute-start.5 = (bf16[2,272,256]{2,1,0:T(8,128)(2,1)S(1)}, bf16[2,272,256]{2,1,0:T(8,128)(2,1)S(1)}, u32[]{:S(2)}, u32[]{:S(2)}) collective-permute-start(bf16[2,272,256]{2,1,0:T(8,128)(2,1)S(1)} %get-tuple-element.88), channel_id=1, source_target_pairs={{0,8},{1,9},{2,10},{3,11},{4,12},{5,13},{6,14},{7,15},{8,0},{9,1},... | collective-permute-start | bytes 835592 | tf_op jit(solution)/shard_map/ppermute | solution.py:501
  19.9 0.7 %copy-start.4 = (f32[2,1024]{1,0:T(2,128)S(1)}, f32[2,1024]{1,0:T(2,128)}, u32[]{:S(2)}) copy-start(f32[2,1024]{1,0:T(2,128)} %refs_4_.1) | copy-start | bytes 24580
  23.7 3.7 %collective-permute-start.4 = (bf16[2,272,256]{2,1,0:T(8,128)(2,1)S(1)}, bf16[2,272,256]{2,1,0:T(8,128)(2,1)S(1)}, u32[]{:S(2)}, u32[]{:S(2)}) collective-permute-start(bf16[2,272,256]{2,1,0:T(8,128)(2,1)S(1)} %get-tuple-element.85.refs_0_), channel_id=1, source_target_pairs={{0,64},{64,0},{1,65},{65,1},{2,66},{66,2},{3,67},{67,3},{4,68},{68... | collective-permute-start | bytes 835592 | tf_op jit(solution)/shard_map/ppermute | solution.py:537
  27.3 2.8 %collective-permute-start.7 = (bf16[2,272,256]{2,1,0:T(8,128)(2,1)S(1)}, bf16[2,272,256]{2,1,0:T(8,128)(2,1)S(1)}, u32[]{:S(2)}, u32[]{:S(2)}) collective-permute-start(bf16[2,272,256]{2,1,0:T(8,128)(2,1)S(1)} %get-tuple-element.94.refs_0_), channel_id=1, source_target_pairs={{0,64},{64,0},{1,65},{65,1},{2,66},{66,2},{3,67},{67,3},{4,68},{68... | collective-permute-start | bytes 835592 | tf_op jit(solution)/shard_map/ppermute | solution.py:537
  27.5 4.1 %collective-permute-start.6 = (bf16[4,272,256]{2,1,0:T(8,128)(2,1)S(1)}, bf16[4,272,256]{2,1,0:T(8,128)(2,1)S(1)}, u32[]{:S(2)}, u32[]{:S(2)}) collective-permute-start(bf16[4,272,256]{2,1,0:T(8,128)(2,1)S(1)} %get-tuple-element.93.refs_0_), channel_id=1, source_target_pairs={{0,64},{64,0},{1,65},{65,1},{2,66},{66,2},{3,67},{67,3},{4,68},{68... | collective-permute-start | bytes 1671176 | tf_op jit(solution)/shard_map/ppermute | solution.py:537
  31.7 7.7 %collective-permute-start.8 = (bf16[272,256]{1,0:T(8,128)(2,1)S(1)}, bf16[272,256]{1,0:T(8,128)(2,1)S(1)}, u32[]{:S(2)}, u32[]{:S(2)}) collective-permute-start(bf16[272,256]{1,0:T(8,128)(2,1)S(1)} %get-tuple-element.99), channel_id=1, source_target_pairs={{0,8},{1,9},{2,10},{3,11},{4,12},{5,13},{6,14},{7,15},{8,0},{9,1},... | collective-permute-start | bytes 417800 | tf_op jit(solution)/shard_map/ppermute | solution.py:501
  39.4 2.3 %collective-permute-start.9 = (bf16[272,256]{1,0:T(8,128)(2,1)S(1)}, bf16[272,256]{1,0:T(8,128)(2,1)S(1)}, u32[]{:S(2)}, u32[]{:S(2)}) collective-permute-start(bf16[272,256]{1,0:T(8,128)(2,1)S(1)} %get-tuple-element.105.refs_0_), channel_id=1, source_target_pairs={{0,64},{64,0},{1,65},{65,1},{2,66},{66,2},{3,67},{67,3},{4,68},{68... | collective-permute-start | bytes 417800 | tf_op jit(solution)/shard_map/ppermute | solution.py:537
  43.1 2.8 %collective-permute-start.11 = (bf16[4,272,256]{2,1,0:T(8,128)(2,1)S(1)}, bf16[4,272,256]{2,1,0:T(8,128)(2,1)S(1)}, u32[]{:S(2)}, u32[]{:S(2)}) collective-permute-start(bf16[4,272,256]{2,1,0:T(8,128)(2,1)S(1)} %get-tuple-element.116.refs_0_), channel_id=1, source_target_pairs={{0,64},{64,0},{1,65},{65,1},{2,66},{66,2},{3,67},{67,3},{4,68},{68... | collective-permute-start | bytes 1671176 | tf_op jit(solution)/shard_map/ppermute | solution.py:537
  43.7 8.0 %collective-permute-start.10 = (bf16[272,256]{1,0:T(8,128)(2,1)S(1)}, bf16[272,256]{1,0:T(8,128)(2,1)S(1)}, u32[]{:S(2)}, u32[]{:S(2)}) collective-permute-start(bf16[272,256]{1,0:T(8,128)(2,1)S(1)} %get-tuple-element.115), channel_id=1, source_target_pairs={{0,56},{1,57},{2,58},{3,59},{4,60},{5,61},{6,62},{7,63},{8,16},{9,... | collective-permute-start | bytes 417800 | tf_op jit(solution)/shard_map/ppermute | solution.py:501
  45.9 5.8 %collective-permute-start.12 = (bf16[272,256]{1,0:T(8,128)(2,1)S(1)}, bf16[272,256]{1,0:T(8,128)(2,1)S(1)}, u32[]{:S(2)}, u32[]{:S(2)}) collective-permute-start(bf16[272,256]{1,0:T(8,128)(2,1)S(1)} %get-tuple-element.120), channel_id=1, source_target_pairs={{0,56},{1,57},{2,58},{3,59},{4,60},{5,61},{6,62},{7,63},{8,16},{9,... | collective-permute-start | bytes 417800 | tf_op jit(solution)/shard_map/ppermute | solution.py:501
  51.8 5.0 %collective-permute-start.13 = (bf16[2,272,256]{2,1,0:T(8,128)(2,1)S(1)}, bf16[2,272,256]{2,1,0:T(8,128)(2,1)S(1)}, u32[]{:S(2)}, u32[]{:S(2)}) collective-permute-start(bf16[2,272,256]{2,1,0:T(8,128)(2,1)S(1)} %get-tuple-element.125.refs_0_), channel_id=1, source_target_pairs={{0,64},{64,0},{1,65},{65,1},{2,66},{66,2},{3,67},{67,3},{4,68},{68... | collective-permute-start | bytes 835592 | tf_op jit(solution)/shard_map/ppermute | solution.py:537

commit v2 on v1

--- a/solution.py
+++ b/solution.py
@@ -389,7 +389,7 @@
     pass
 
 
-def k_fourth(mine, other, w, bias, cx_in, h_in, a_in, b_in, acc_a, acc_b, cx, h, out, s):
+def k_fourth(mine, other, w, bias, cx_in, h_in, a_in, b_in, acc_a, acc_b, cx, h, s):
     halo(s, mine[...], other[...])
 
     def work(acc, off, layer):
@@ -402,8 +402,6 @@
     @core_is(1)
     def _():
         work(acc_a, 0, 1)
-
-    out[...] = h[my_row(1)]
 
 
 def k_fifth(h, w, acc_in, acc, s):
@@ -417,14 +415,11 @@
             inner(acc, w, s, 256, 0, r, 0, COLS, False)
 
 
-def k_lent(recv, out):
-    out[...] = recv[my_row(1)]
-
-
-def k_join(own, lent, out):
+def k_pick_two(h, recv, out):
+    r = my_row(1)
     core = lax.axis_index("layer")
-    out[core] = own[...]
-    out[1 - core] = lent[...]
+    out[core] = h[r]
+    out[1 - core] = recv[r]
 
 
 def k_sixth(recv, w, s1, acc_in, acc, s):
@@ -453,41 +448,52 @@
                     finish_center(acc, bias, done, n, cx, hv, cv)
 
 
-def k_last(mine, other, cx, w, bias, hv_in, cv_in, acc_in, acc, hv, cv, ho, co, s, sem):
-    def out(r):
+def last_row(rows, low, acc, w, bias, cx, hv, cv, s):
+    r = jnp.where(low, ROWS - 1, 0)
+    first = jnp.where(low, 6, 0)
+    real = jnp.where(low, inside("gy", 1), inside("gy", -1))
+    for i in range(2):
+        x = rows[i].astype(f32) * real
+        for dx, y in ((0, pltpu.roll(x, 1, 0)), (1, x), (2, pltpu.roll(x, EXT - 1, 0))):
+            s[i, dx] = y[PAD : PAD + COLS].astype(bf16)
+    for n in BLOCKS:
+        total = acc[r, 0:COLS, block(n)]
+        for dx in range(3):
+            for i in range(2):
+                total = taps(w, n, s[i, dx], 256 * i, first + dx, total)
+        acc[r, 0:COLS, block(n)] = total
+    for n in BLOCKS:
+        finish_center(acc, bias, r, n, cx, hv, cv)
+
+
+def k_mine(mine, cx, w, bias, hv_in, cv_in, acc_in, acc, hv, cv, s):
+    @core_is(1)
+    def _():
+        last_row(mine, below(1), acc, w, bias, cx, hv, cv, s)
+
+
+def k_last(other, cx, w, bias, hv_in, cv_in, acc_in, acc, hv, cv, ho, co, s, sem):
+    rows = (1, 2, my_row(1), ROWS - 1 - my_row(1))
+
+    def out(k):
+        r = rows[k]
         return (
-            pltpu.make_async_copy(hv.at[r], ho.at[0, r], sem.at[0, r]),
-            pltpu.make_async_copy(cv.at[r], co.at[0, r], sem.at[1, r]),
+            pltpu.make_async_copy(hv.at[r], ho.at[0, r], sem.at[0, k]),
+            pltpu.make_async_copy(cv.at[r], co.at[0, r], sem.at[1, k]),
         )
 
-    def send(r):
-        for c in out(r):
+    for k in range(3):
+        for c in out(k):
             c.start()
 
-    for r in (1, 2):
-        send(r)
-
-    @core_is(1)
-    def _():
-        halo(s.at[0], mine[0], other[0], build_center, 1)
-        halo(s.at[1], mine[1], other[1], build_center, 1)
-        for end in (0, 1):
-            for n in BLOCKS:
-                outer(acc, w, ((s.at[0], 0), (s.at[1], 256)), n, end, COLS)
-                if end:
-                    finish_center(acc, bias, 0, n, cx, hv, cv)
-        send(0)
-        for n in BLOCKS:
-            finish_center(acc, bias, ROWS - 1, n, cx, hv, cv)
-        send(ROWS - 1)
-
-    @core_is(0)
-    def _():
-        for r in (0, 3):
-            send(r)
-
-    for r in range(ROWS):
-        for c in out(r):
+    @core_is(1)
+    def _():
+        last_row(other, jnp.logical_not(below(1)), acc, w, bias, cx, hv, cv, s)
+
+    for c in out(3):
+        c.start()
+    for k in range(ROWS):
+        for c in out(k):
             c.wait()
 
 
@@ -595,9 +601,9 @@
     mine = hold(mine)
     other = swap_cores(mine)
     acc_a, acc_b = call(k_ends, [sums, sums], [w, s, acc_a, acc_b], aliases={2: 0, 3: 1}, part=0.2)
-    acc_a, acc_b, cx, h, out = call(
+    acc_a, acc_b, cx, h = call(
         k_fourth,
-        [sums, sums, tile32, tile, row],
+        [sums, sums, tile32, tile],
         [mine, other, w, bias, cx, h2, acc_a, acc_b],
         aliases={4: 2, 5: 3, 6: 0, 7: 1},
         scratch=[pltpu.VMEM(PAIR, bf16)],
@@ -605,14 +611,22 @@
     )
 
     recv = swap_cores(h)
-    mine = swap_rows(out, 1)
     acc_b, s = call(k_fifth, [sums, vm(CENTER, bf16)], [h, w, acc_b], aliases={2: 0}, part=0.22)
-    mine_lent = swap_rows(call(k_lent, [row], [recv])[0], 1)
+    mine = swap_rows(call(k_pick_two, [two_rows], [h, recv])[0], 1)
     hv, cv = vm((ROWS, COLS, CH), bf16), vm((ROWS, COLS, CH), f32)
     acc_b, s = call(k_sixth, [sums, vm(CENTER, bf16)], [recv, w, s, acc_b], aliases={3: 0}, part=0.45)
-    (mine,) = call(k_join, [two_rows], [mine, mine_lent])
+    acc_b, hid, cell = call(k_seventh, [sums, hv, cv], [h, cx, w, bias, s, acc_b], aliases={5: 0}, part=0.25)
+    mine = hold(mine)
     other = swap_cores(mine)
-    acc_b, hid, cell = call(k_seventh, [sums, hv, cv], [h, cx, w, bias, s, acc_b], aliases={5: 0}, part=0.25)
+    side = pltpu.VMEM((2, 3, COLS, CH), bf16)
+    acc_b, hid, cell = call(
+        k_mine,
+        [sums, hv, cv],
+        [mine, cx, w, bias, hid, cell, acc_b],
+        aliases={4: 1, 5: 2, 6: 0},
+        scratch=[side],
+        part=0.2,
+    )
     _, _, _, ho, co = call(
         k_last,
         [
@@ -622,11 +636,11 @@
             jax.ShapeDtypeStruct((1, ROWS, COLS, CH), bf16),
             jax.ShapeDtypeStruct((1, ROWS, COLS, CH), f32),
         ],
-        [mine, other, cx, w, bias, hid, cell, acc_b],
-        aliases={5: 1, 6: 2, 7: 0},
+        [other, cx, w, bias, hid, cell, acc_b],
+        aliases={4: 1, 5: 2, 6: 0},
         far_out=(3, 4),
-        scratch=[pltpu.VMEM((2, 3, 2, COLS, CH), bf16), pltpu.SemaphoreType.DMA((2, ROWS))],
-        part=0.3,
+        scratch=[side, pltpu.SemaphoreType.DMA((2, ROWS))],
+        part=0.2,
     )
     return ho, co
 

time: 60.6 us -> 58.4 us (0.964)
  starting transfers between devices: 25.5 us -> 23 us
    ppermute x5 -> x4, starting transfers between devices: 11.2 us -> 9.75 us  [swap_rows(): return lax.ppermute(x, ('layer', 'gy', 'gx'), pairs)]
    ppermute x7, starting transfers between devices: 8.18 us -> 7.12 us  [swap_cores(): return lax.ppermute(x, 'layer', swap)]
    pallas_call x23 -> x24, Pallas kernels: 26.9 us -> 27.1 us  [__call__(): pl.pallas_call(kernel, in_specs=[HBM if i in far else ANYV for i in range...]
    ppermute x5 -> x4, waiting for transfers between devices: 5.52 us -> 5.53 us  [swap_rows(): return lax.ppermute(x, ('layer', 'gy', 'gx'), pairs)]
  transfers between devices with their start and end apart: 14 -> 13, of which waited for: 4 -> 5; matrix products, arithmetic and copies ran while one was open for 0% -> 0% of each run, Pallas kernels for 34% -> 38%
where the time goes in v2:
time: 58.4 us; the launch traced here: 58.3 us
  Pallas kernels  27.1 us (46%)
  starting transfers between devices  23 us (39%)
  waiting for transfers between devices  6.22 us (11%)
  between operations  1.03 us (2%)
  local copies, waits for them, and re-layouts  0.94 us (2%)
    pallas_call x24, Pallas kernels, __call__(): pl.pallas_call(kernel, in_specs=[HBM if i in far else ANYV for i in range...  27.1 us
    ppermute x4, starting transfers between devices, swap_rows(): return lax.ppermute(x, ('layer', 'gy', 'gx'), pairs)  9.75 us
    ppermute x7, starting transfers between devices, swap_cores(): return lax.ppermute(x, 'layer', swap)  7.12 us
    ppermute x4, waiting for transfers between devices, swap_rows(): return lax.ppermute(x, ('layer', 'gy', 'gx'), pairs)  5.53 us
    ppermute x1, starting transfers between devices, both_ways(): from_low = lax.ppermute(to_high, axis, [(i, (i + 1) % n) for i in range(n)])  3.81 us
    ppermute x1, starting transfers between devices, both_ways(): from_high = lax.ppermute(to_low, axis, [(i, (i - 1) % n) for i in range(n)])  2.28 us
  transfers between devices with their start and end apart: 13, of which 5 were waited for; matrix products, arithmetic and copies ran while one was open for 0% of the time, Pallas kernels for 38%

profile of v2, /device:TPU:1, one launch (start us, length us, event | category | flops | bytes accessed | tf_op | source)
XLA Modules:
  0.0 58.3 jit_solution(2960048108044845084)
XLA Ops:
  0.6 1.2 %shard_map.68 = (bf16[20,8,256]{2,1,0:T(8,128)(2,1)S(1)}, bf16[20,8,256]{2,1,0:T(8,128)(2,1)S(1)}, f32[8,128]{1,0:T(8,128)S(1)}) custom-call(bf16[2,4,256,256]{3,2,1,0:T(8,128)(2,1)} %refs_0_.11, bf16[1,4,256,256]{3,2,1,0:T(8,128)(2,1)} %refs_1_.5, f32[1,4,256,256]{3,2,1,0:T(8,128)} %refs_1_.4), custom_call_target="tpu_custom_call" | custom-call | flops 19327352832 | bytes 1048576 | tf_op jit(solution)/shard_map/pallas_call | solution.py:48
  1.8 3.8 %collective-permute-start = (bf16[20,8,256]{2,1,0:T(8,128)(2,1)S(1)}, bf16[20,8,256]{2,1,0:T(8,128)(2,1)S(1)}, u32[]{:S(2)}, u32[]{:S(2)}) collective-permute-start(bf16[20,8,256]{2,1,0:T(8,128)(2,1)S(1)} %get-tuple-element.72), channel_id=1, source_target_pairs={{0,1},{1,2},{2,3},{3,4},{4,5},{5,6},{6,7},{7,0},{8,9},{9,10},{10,1... | collective-permute-start | bytes 245768 | tf_op jit(solution)/shard_map/ppermute | solution.py:512
  5.7 2.3 %collective-permute-start.1 = (bf16[20,8,256]{2,1,0:T(8,128)(2,1)S(1)}, bf16[20,8,256]{2,1,0:T(8,128)(2,1)S(1)}, u32[]{:S(2)}, u32[]{:S(2)}) collective-permute-start(bf16[20,8,256]{2,1,0:T(8,128)(2,1)S(1)} %get-tuple-element.73), channel_id=1, source_target_pairs={{0,7},{1,0},{2,1},{3,2},{4,3},{5,4},{6,5},{7,6},{8,15},{9,8},{10,9... | collective-permute-start | bytes 245768 | tf_op jit(solution)/shard_map/ppermute | solution.py:513
  7.9 4.4 %shard_map.69 = (f32[4,272,1024]{2,1,0:T(8,128)S(1)}, f32[8,128]{1,0:T(8,128)S(1)}) custom-call(bf16[1,4,256,256]{3,2,1,0:T(8,128)(2,1)S(1)} %copy-done.1, bf16[9,512,1024]{2,1,0:T(8,128)(2,1)S(1)} %bitcast.1, f32[8,128]{1,0:T(8,128)S(1)} %get-tuple-element.74.refs_2_), custom_call_target="tpu_custom_call" | custom-call | flops 3865470464 | bytes 1048576 | tf_op jit(solution)/shard_map/pallas_call | solution.py:48
  12.4 1.1 %collective-permute-start.2 = (bf16[272,256]{1,0:T(8,128)(2,1)S(1)}, bf16[272,256]{1,0:T(8,128)(2,1)S(1)}, u32[]{:S(2)}, u32[]{:S(2)}) collective-permute-start(bf16[272,256]{1,0:T(8,128)(2,1)S(1)} %get-tuple-element.76), channel_id=1, source_target_pairs={{0,64},{64,0},{1,65},{65,1},{2,66},{66,2},{3,67},{67,3},{4,68},{68... | collective-permute-start | bytes 417800 | tf_op jit(solution)/shard_map/ppermute | solution.py:543
  13.6 0.9 %shard_map.71 = (f32[4,272,1024]{2,1,0:T(8,128)S(1)}, f32[4,272,256]{2,1,0:T(8,128)S(1)}, f32[8,128]{1,0:T(8,128)S(1)}) custom-call(bf16[1,4,256,256]{3,2,1,0:T(8,128)(2,1)S(1)} %copy-done.1, f32[1,4,256,256]{3,2,1,0:T(8,128)S(1)} %copy-done.2, bf16[9,512,1024]{2,1,0:T(8,128)(2,1)S(1)} %bitcast.2, ...), custom_call_target="tpu_custom_call", output_to_operand_aliasing={{0}: (5, {})} | custom-call | flops 966367616 | bytes 1048576 | tf_op jit(solution)/shard_map/pallas_call | solution.py:48
  14.6 0.2 copy-done.3
  14.8 0.1 shard_map.72
  14.9 4.9 %collective-permute-start.3 = (bf16[2,272,256]{2,1,0:T(8,128)(2,1)S(1)}, bf16[2,272,256]{2,1,0:T(8,128)(2,1)S(1)}, u32[]{:S(2)}, u32[]{:S(2)}) collective-permute-start(bf16[2,272,256]{2,1,0:T(8,128)(2,1)S(1)} %get-tuple-element.80), channel_id=1, source_target_pairs={{0,8},{1,9},{2,10},{3,11},{4,12},{5,13},{6,14},{7,15},{8,0},{9,1},... | collective-permute-start | bytes 835592 | tf_op jit(solution)/shard_map/ppermute | solution.py:507
  19.8 0.1 collective-permute-start.5
  19.9 0.7 %copy-done.4 = f32[2,1024]{1,0:T(2,128)S(1)} copy-done((f32[2,1024]{1,0:T(2,128)S(1)}, f32[2,1024]{1,0:T(2,128)}, u32[]{:S(2)}) %copy-start.4) | copy-done | bytes 8216
  20.6 3.1 %collective-permute-done.3.refs_0_ = bf16[2,272,256]{2,1,0:T(8,128)(2,1)S(1)} collective-permute-done((bf16[2,272,256]{2,1,0:T(8,128)(2,1)S(1)}, bf16[2,272,256]{2,1,0:T(8,128)(2,1)S(1)}, u32[]{:S(2)}, u32[]{:S(2)}) %collective-permute-start.3) | collective-permute-done | bytes 278560 | tf_op jit(solution)/shard_map/ppermute | solution.py:507
  23.7 1.2 %collective-permute-start.4 = (bf16[2,272,256]{2,1,0:T(8,128)(2,1)S(1)}, bf16[2,272,256]{2,1,0:T(8,128)(2,1)S(1)}, u32[]{:S(2)}, u32[]{:S(2)}) collective-permute-start(bf16[2,272,256]{2,1,0:T(8,128)(2,1)S(1)} %get-tuple-element.88.refs_0_), channel_id=1, source_target_pairs={{0,64},{64,0},{1,65},{65,1},{2,66},{66,2},{3,67},{67,3},{4,68},{68... | collective-permute-start | bytes 835592 | tf_op jit(solution)/shard_map/ppermute | solution.py:543
  24.9 2.4 %collective-permute-done.5.refs_0_ = bf16[2,272,256]{2,1,0:T(8,128)(2,1)S(1)} collective-permute-done((bf16[2,272,256]{2,1,0:T(8,128)(2,1)S(1)}, bf16[2,272,256]{2,1,0:T(8,128)(2,1)S(1)}, u32[]{:S(2)}, u32[]{:S(2)}) %collective-permute-start.5) | collective-permute-done | bytes 278560 | tf_op jit(solution)/shard_map/ppermute | solution.py:507
  27.4 0.1 shard_map.78
  27.5 2.6 %collective-permute-start.6 = (bf16[4,272,256]{2,1,0:T(8,128)(2,1)S(1)}, bf16[4,272,256]{2,1,0:T(8,128)(2,1)S(1)}, u32[]{:S(2)}, u32[]{:S(2)}) collective-permute-start(bf16[4,272,256]{2,1,0:T(8,128)(2,1)S(1)} %get-tuple-element.96.refs_0_), channel_id=1, source_target_pairs={{0,64},{64,0},{1,65},{65,1},{2,66},{66,2},{3,67},{67,3},{4,68},{68... | collective-permute-start | bytes 1671176 | tf_op jit(solution)/shard_map/ppermute | solution.py:543
  30.1 1.1 %shard_map.79 = (f32[4,272,1024]{2,1,0:T(8,128)S(1)}, f32[4,272,1024]{2,1,0:T(8,128)S(1)}, f32[8,128]{1,0:T(8,128)S(1)}) custom-call(bf16[2,272,256]{2,1,0:T(8,128)(2,1)S(1)} %get-tuple-element.97.refs_0_, bf16[2,272,256]{2,1,0:T(8,128)(2,1)S(1)} %collective-permute-done.7.refs_1_, ...), custom_call_target="tpu_custom_call", output_to_operand_aliasing={{0}: (3, {}), {1}: (4, {})} | custom-call | flops 4831838208 | bytes 1048576 | tf_op jit(solution)/shard_map/pallas_call | solution.py:48
  31.1 0.5 collective-permute-done.6.refs_1_
  31.7 4.6 %collective-permute-start.8 = (bf16[272,256]{1,0:T(8,128)(2,1)S(1)}, bf16[272,256]{1,0:T(8,128)(2,1)S(1)}, u32[]{:S(2)}, u32[]{:S(2)}) collective-permute-start(bf16[272,256]{1,0:T(8,128)(2,1)S(1)} %get-tuple-element.102), channel_id=1, source_target_pairs={{0,8},{1,9},{2,10},{3,11},{4,12},{5,13},{6,14},{7,15},{8,0},{9,1},... | collective-permute-start | bytes 417800 | tf_op jit(solution)/shard_map/ppermute | solution.py:507
  36.3 3.0 %shard_map.81 = (f32[4,272,1024]{2,1,0:T(8,128)S(1)}, f32[4,272,1024]{2,1,0:T(8,128)S(1)}, f32[4,272,256]{2,1,0:T(8,128)S(1)}, bf16[4,272,256]{2,1,0:T(8,128)(2,...) custom-call(bf16[4,272,256]{2,1,0:T(8,128)(2,1)S(1)} %get-tuple-elem, ...), custom_call_target="tpu_custom_call", output_to_operand_aliasing={{2}: (4, {}), {0}: (5, {}), {1}: (6, {})} | custom-call | flops 2415919104 | bytes 1048576 | tf_op jit(solution)/shard_map/pallas_call | solution.py:48
  39.3 0.1 collective-permute-start.9
  39.4 2.2 %shard_map.83 = (f32[4,272,1024]{2,1,0:T(8,128)S(1)}, f32[4,272,1024]{2,1,0:T(8,128)S(1)}, f32[8,128]{1,0:T(8,128)S(1)}) custom-call(bf16[9,512,1024]{2,1,0:T(8,128)(2,1)S(1)} %bitcast.9, bf16[3,4,272,256]{3,2,1,0:T(8,128)(2,1)S(1)} %get-tuple-element.111.refs_1_, ...), custom_call_target="tpu_custom_call", output_to_operand_aliasing={{0}: (2, {}), {1}: (3, {})} | custom-call | flops 1932735232 | bytes 1048576 | tf_op jit(solution)/shard_map/pallas_call | solution.py:48
  41.6 1.4 %shard_map.84 = (f32[4,272,1024]{2,1,0:T(8,128)S(1)}, f32[4,272,1024]{2,1,0:T(8,128)S(1)}, f32[4,272,256]{2,1,0:T(8,128)S(1)}, bf16[4,272,256]{2,1,0:T(8,128)(2,1)S(1)}, f32[8,128]{1,0:T(8,128)S(1)}) custom-call(bf16[272,256]{1,0:T(8,128)(2,1)S(1)} %get-tuple-element.108.refs_0_, ...), custom_call_target="tpu_custom_call", output_to_operand_aliasing={{2}: (4, {}), {3}: (5, {}), {0}: (6, {}), {1}: (7, {})} | custom-call | flops 1932735232 | bytes 1048576 | tf_op jit(solution)/shard_map/pallas_call | solution.py:48
  43.1 0.6 %collective-permute-start.10 = (bf16[4,272,256]{2,1,0:T(8,128)(2,1)S(1)}, bf16[4,272,256]{2,1,0:T(8,128)(2,1)S(1)}, u32[]{:S(2)}, u32[]{:S(2)}) collective-permute-start(bf16[4,272,256]{2,1,0:T(8,128)(2,1)S(1)} %get-tuple-element.118.refs_0_), channel_id=1, source_target_pairs={{0,64},{64,0},{1,65},{65,1},{2,66},{66,2},{3,67},{67,3},{4,68},{68... | collective-permute-start | bytes 1671176 | tf_op jit(solution)/shard_map/ppermute | solution.py:543
  43.7 2.2 %shard_map.85 = (f32[4,272,1024]{2,1,0:T(8,128)S(1)}, bf16[3,4,256,256]{3,2,1,0:T(8,128)(2,1)S(1)}, f32[8,128]{1,0:T(8,128)S(1)}) custom-call(bf16[4,272,256]{2,1,0:T(8,128)(2,1)S(1)} %get-tuple-element.118.refs_0_, bf16[9,512,1024]{2,1,0:T(8,128)(2,1)S(1)} %bitcast.11, ...), custom_call_target="tpu_custom_call", output_to_operand_aliasing={{0}: (2, {})} | custom-call | flops 2126008832 | bytes 1048576 | tf_op jit(solution)/shard_map/pallas_call | solution.py:48
  46.0 0.1 collective-permute-start.11
  46.1 4.3 %shard_map.87 = (f32[4,272,1024]{2,1,0:T(8,128)S(1)}, bf16[3,4,256,256]{3,2,1,0:T(8,128)(2,1)S(1)}, f32[8,128]{1,0:T(8,128)S(1)}) custom-call(bf16[4,272,256]{2,1,0:T(8,128)(2,1)S(1)} %collective-permute-done.10.refs_1_.refs_0_, bf16[9,512,1024]{2,1,0:T(8,128)(2,1)S(1)} %bitcast.12, ...), custom_call_target="tpu_custom_call", output_to_operand_aliasing={{0}: (3, {})} | custom-call | flops 4348654592 | bytes 1048576 | tf_op jit(solution)/shard_map/pallas_call | solution.py:48
  50.4 2.5 %shard_map.88 = (f32[4,272,1024]{2,1,0:T(8,128)S(1)}, bf16[4,256,256]{2,1,0:T(8,128)(2,1)S(1)}, f32[4,256,256]{2,1,0:T(8,128)S(1)}, f32[8,128]{1,0:T(8,128)S(1)}) custom-call(bf16[4,272,256]{2,1,0:T(8,128)(2,1)S(1)} %get-tuple-element.118.refs_0_, f32[4,272,256]{2,1,0:T(8,128)S(1)} %get-tuple-element.123.refs_1_, ...), custom_call_target="tpu_custom_call", output_to_operand_aliasing={{0}: (5, {})} | custom-call | flops 2415919104 | bytes 1048576 | tf_op jit(solution)/shard_map/pallas_call | solution.py:48
  53.0 1.5 %collective-permute-start.12 = (bf16[2,272,256]{2,1,0:T(8,128)(2,1)S(1)}, bf16[2,272,256]{2,1,0:T(8,128)(2,1)S(1)}, u32[]{:S(2)}, u32[]{:S(2)}) collective-permute-start(bf16[2,272,256]{2,1,0:T(8,128)(2,1)S(1)} %get-tuple-element.131.refs_0_), channel_id=1, source_target_pairs={{0,64},{64,0},{1,65},{65,1},{2,66},{66,2},{3,67},{67,3},{4,68},{68... | collective-permute-start | bytes 835592 | tf_op jit(solution)/shard_map/ppermute | solution.py:543
  54.4 1.1 %shard_map.90 = (f32[4,272,1024]{2,1,0:T(8,128)S(1)}, bf16[4,256,256]{2,1,0:T(8,128)(2,1)S(1)}, f32[4,256,256]{2,1,0:T(8,128)S(1)}, f32[8,128]{1,0:T(8,128)S(1)}) custom-call(bf16[2,272,256]{2,1,0:T(8,128)(2,1)S(1)} %get-tuple-element.131.refs_0_, ...), custom_call_target="tpu_custom_call", output_to_operand_aliasing={{1}: (4, {}), {2}: (5, {}), {0}: (6, {})} | custom-call | flops 1932735232 | bytes 1048576 | tf_op jit(solution)/shard_map/pallas_call | solution.py:48
  55.5 0.1 collective-permute-done.12.refs_0_
  55.6 2.5 %shard_map.91 = (f32[4,272,1024]{2,1,0:T(8,128)S(1)}, bf16[4,256,256]{2,1,0:T(8,128)(2,1)S(1)}, f32[4,256,256]{2,1,0:T(8,128)S(1)}, bf16[1,4,256,256]{3,2,1,0:T(...) custom-call(bf16[2,272,256]{2,1,0:T(8,128)(2,1)S(1)} %collective-per, ...), custom_call_target="tpu_custom_call", output_to_operand_aliasing={{1}: (4, {}), {2}: (5, {}), {0}: (6, {})} | custom-call | flops 1932735232 | bytes 1048576 | tf_op jit(solution)/shard_map/pallas_call | solution.py:48
  (28 shorter events, 0.3 us)
Async XLA Ops:
  0.6 7.3 %copy-start.1 = (bf16[1,4,256,256]{3,2,1,0:T(8,128)(2,1)S(1)}, bf16[1,4,256,256]{3,2,1,0:T(8,128)(2,1)}, u32[]{:S(2)}) copy-start(bf16[1,4,256,256]{3,2,1,0:T(8,128)(2,1)} %refs_1_.5) | copy-start | bytes 1572868
  0.6 7.3 %copy-start = (bf16[1,4608,1024]{2,1,0:T(8,128)(2,1)S(1)}, bf16[1,4608,1024]{2,1,0:T(8,128)(2,1)}, u32[]{:S(2)}) copy-start(bf16[1,4608,1024]{2,1,0:T(8,128)(2,1)} %param.8) | copy-start | bytes 28311556
  1.8 10.5 %collective-permute-start = (bf16[20,8,256]{2,1,0:T(8,128)(2,1)S(1)}, bf16[20,8,256]{2,1,0:T(8,128)(2,1)S(1)}, u32[]{:S(2)}, u32[]{:S(2)}) collective-permute-start(bf16[20,8,256]{2,1,0:T(8,128)(2,1)S(1)} %get-tuple-element.72), channel_id=1, source_target_pairs={{0,1},{1,2},{2,3},{3,4},{4,5},{5,6},{6,7},{7,0},{8,9},{9,10},{10,1... | collective-permute-start | bytes 245768 | tf_op jit(solution)/shard_map/ppermute | solution.py:512
  5.7 6.7 %collective-permute-start.1 = (bf16[20,8,256]{2,1,0:T(8,128)(2,1)S(1)}, bf16[20,8,256]{2,1,0:T(8,128)(2,1)S(1)}, u32[]{:S(2)}, u32[]{:S(2)}) collective-permute-start(bf16[20,8,256]{2,1,0:T(8,128)(2,1)S(1)} %get-tuple-element.73), channel_id=1, source_target_pairs={{0,7},{1,0},{2,1},{3,2},{4,3},{5,4},{6,5},{7,6},{8,15},{9,8},{10,9... | collective-permute-start | bytes 245768 | tf_op jit(solution)/shard_map/ppermute | solution.py:513
  7.9 5.6 %copy-start.2 = (f32[1,4,256,256]{3,2,1,0:T(8,128)S(1)}, f32[1,4,256,256]{3,2,1,0:T(8,128)}, u32[]{:S(2)}) copy-start(f32[1,4,256,256]{3,2,1,0:T(8,128)} %refs_1_.4) | copy-start | bytes 3145732
  12.4 2.1 %collective-permute-start.2 = (bf16[272,256]{1,0:T(8,128)(2,1)S(1)}, bf16[272,256]{1,0:T(8,128)(2,1)S(1)}, u32[]{:S(2)}, u32[]{:S(2)}) collective-permute-start(bf16[272,256]{1,0:T(8,128)(2,1)S(1)} %get-tuple-element.76), channel_id=1, source_target_pairs={{0,64},{64,0},{1,65},{65,1},{2,66},{66,2},{3,67},{67,3},{4,68},{68... | collective-permute-start | bytes 417800 | tf_op jit(solution)/shard_map/ppermute | solution.py:543
  13.6 1.2 %copy-start.3 = (bf16[2,4,256,256]{3,2,1,0:T(8,128)(2,1)S(1)}, bf16[2,4,256,256]{3,2,1,0:T(8,128)(2,1)}, u32[]{:S(2)}) copy-start(bf16[2,4,256,256]{3,2,1,0:T(8,128)(2,1)} %refs_0_.11) | copy-start | bytes 3145732
  14.9 8.9 %collective-permute-start.3 = (bf16[2,272,256]{2,1,0:T(8,128)(2,1)S(1)}, bf16[2,272,256]{2,1,0:T(8,128)(2,1)S(1)}, u32[]{:S(2)}, u32[]{:S(2)}) collective-permute-start(bf16[2,272,256]{2,1,0:T(8,128)(2,1)S(1)} %get-tuple-element.80), channel_id=1, source_target_pairs={{0,8},{1,9},{2,10},{3,11},{4,12},{5,13},{6,14},{7,15},{8,0},{9,1},... | collective-permute-start | bytes 835592 | tf_op jit(solution)/shard_map/ppermute | solution.py:507
  19.8 7.5 %collective-permute-start.5 = (bf16[2,272,256]{2,1,0:T(8,128)(2,1)S(1)}, bf16[2,272,256]{2,1,0:T(8,128)(2,1)S(1)}, u32[]{:S(2)}, u32[]{:S(2)}) collective-permute-start(bf16[2,272,256]{2,1,0:T(8,128)(2,1)S(1)} %get-tuple-element.91), channel_id=1, source_target_pairs={{0,8},{1,9},{2,10},{3,11},{4,12},{5,13},{6,14},{7,15},{8,0},{9,1},... | collective-permute-start | bytes 835592 | tf_op jit(solution)/shard_map/ppermute | solution.py:507
  19.9 0.7 %copy-start.4 = (f32[2,1024]{1,0:T(2,128)S(1)}, f32[2,1024]{1,0:T(2,128)}, u32[]{:S(2)}) copy-start(f32[2,1024]{1,0:T(2,128)} %refs_3_.11) | copy-start | bytes 24580
  23.7 3.6 %collective-permute-start.4 = (bf16[2,272,256]{2,1,0:T(8,128)(2,1)S(1)}, bf16[2,272,256]{2,1,0:T(8,128)(2,1)S(1)}, u32[]{:S(2)}, u32[]{:S(2)}) collective-permute-start(bf16[2,272,256]{2,1,0:T(8,128)(2,1)S(1)} %get-tuple-element.88.refs_0_), channel_id=1, source_target_pairs={{0,64},{64,0},{1,65},{65,1},{2,66},{66,2},{3,67},{67,3},{4,68},{68... | collective-permute-start | bytes 835592 | tf_op jit(solution)/shard_map/ppermute | solution.py:543
  27.3 2.8 %collective-permute-start.7 = (bf16[2,272,256]{2,1,0:T(8,128)(2,1)S(1)}, bf16[2,272,256]{2,1,0:T(8,128)(2,1)S(1)}, u32[]{:S(2)}, u32[]{:S(2)}) collective-permute-start(bf16[2,272,256]{2,1,0:T(8,128)(2,1)S(1)} %get-tuple-element.97.refs_0_), channel_id=1, source_target_pairs={{0,64},{64,0},{1,65},{65,1},{2,66},{66,2},{3,67},{67,3},{4,68},{68... | collective-permute-start | bytes 835592 | tf_op jit(solution)/shard_map/ppermute | solution.py:543
  27.5 4.1 %collective-permute-start.6 = (bf16[4,272,256]{2,1,0:T(8,128)(2,1)S(1)}, bf16[4,272,256]{2,1,0:T(8,128)(2,1)S(1)}, u32[]{:S(2)}, u32[]{:S(2)}) collective-permute-start(bf16[4,272,256]{2,1,0:T(8,128)(2,1)S(1)} %get-tuple-element.96.refs_0_), channel_id=1, source_target_pairs={{0,64},{64,0},{1,65},{65,1},{2,66},{66,2},{3,67},{67,3},{4,68},{68... | collective-permute-start | bytes 1671176 | tf_op jit(solution)/shard_map/ppermute | solution.py:543
  31.7 7.6 %collective-permute-start.8 = (bf16[272,256]{1,0:T(8,128)(2,1)S(1)}, bf16[272,256]{1,0:T(8,128)(2,1)S(1)}, u32[]{:S(2)}, u32[]{:S(2)}) collective-permute-start(bf16[272,256]{1,0:T(8,128)(2,1)S(1)} %get-tuple-element.102), channel_id=1, source_target_pairs={{0,8},{1,9},{2,10},{3,11},{4,12},{5,13},{6,14},{7,15},{8,0},{9,1},... | collective-permute-start | bytes 417800 | tf_op jit(solution)/shard_map/ppermute | solution.py:507
  39.3 2.3 %collective-permute-start.9 = (bf16[272,256]{1,0:T(8,128)(2,1)S(1)}, bf16[272,256]{1,0:T(8,128)(2,1)S(1)}, u32[]{:S(2)}, u32[]{:S(2)}) collective-permute-start(bf16[272,256]{1,0:T(8,128)(2,1)S(1)} %get-tuple-element.108.refs_0_), channel_id=1, source_target_pairs={{0,64},{64,0},{1,65},{65,1},{2,66},{66,2},{3,67},{67,3},{4,68},{68... | collective-permute-start | bytes 417800 | tf_op jit(solution)/shard_map/ppermute | solution.py:543
  43.1 2.9 %collective-permute-start.10 = (bf16[4,272,256]{2,1,0:T(8,128)(2,1)S(1)}, bf16[4,272,256]{2,1,0:T(8,128)(2,1)S(1)}, u32[]{:S(2)}, u32[]{:S(2)}) collective-permute-start(bf16[4,272,256]{2,1,0:T(8,128)(2,1)S(1)} %get-tuple-element.118.refs_0_), channel_id=1, source_target_pairs={{0,64},{64,0},{1,65},{65,1},{2,66},{66,2},{3,67},{67,3},{4,68},{68... | collective-permute-start | bytes 1671176 | tf_op jit(solution)/shard_map/ppermute | solution.py:543
  46.0 6.9 %collective-permute-start.11 = (bf16[2,272,256]{2,1,0:T(8,128)(2,1)S(1)}, bf16[2,272,256]{2,1,0:T(8,128)(2,1)S(1)}, u32[]{:S(2)}, u32[]{:S(2)}) collective-permute-start(bf16[2,272,256]{2,1,0:T(8,128)(2,1)S(1)} %get-tuple-element.122), channel_id=1, source_target_pairs={{0,56},{1,57},{2,58},{3,59},{4,60},{5,61},{6,62},{7,63},{8,16},{9,... | collective-permute-start | bytes 835592 | tf_op jit(solution)/shard_map/ppermute | solution.py:507
  53.0 2.6 %collective-permute-start.12 = (bf16[2,272,256]{2,1,0:T(8,128)(2,1)S(1)}, bf16[2,272,256]{2,1,0:T(8,128)(2,1)S(1)}, u32[]{:S(2)}, u32[]{:S(2)}) collective-permute-start(bf16[2,272,256]{2,1,0:T(8,128)(2,1)S(1)} %get-tuple-element.131.refs_0_), channel_id=1, source_target_pairs={{0,64},{64,0},{1,65},{65,1},{2,66},{66,2},{3,67},{67,3},{4,68},{68... | collective-permute-start | bytes 835592 | tf_op jit(solution)/shard_map/ppermute | solution.py:543
